TPU v7x, 128 devices: a whole 4x4x4 slice. The times are simulated.
128 devices in a mesh: sx: 8 (over z, core), sy: 8 (over y, x_lo), sample: 2 (over x_hi).
Axes of the slice: x: 4 (x_hi: 2, x_lo: 2; x = x_hi * 2 + x_lo), y: 4, z: 4, core: 2. Of those that a mesh axis runs over, the one named last changes fastest.
Arguments:
- inputs: bfloat16 [2, 192, 2, 128, 1024], P('sample', None, None, 'sx', 'sy'), may hold values from -6 to 6
- cotangent: bfloat16 [2, 192, 2, 128, 1024], P('sample', None, None, 'sx', 'sy'), may hold values from -6 to 6
- depth_kernel: float32 [192, 27], replicated, may hold values from -1.25 to 1.25
- mix_in: bfloat16 [192, 192], replicated, may hold values from -0.4375 to 0.4375
- mix_bias: float32 [192], replicated, may hold values from -3 to 3
- mix_out: bfloat16 [192, 192], replicated, may hold values from -0.4375 to 0.4375
Outputs:
- input_grad: bfloat16 [2, 192, 2, 128, 1024], P('sample', None, None, 'sx', 'sy')
- kernel_grad: float32 [192, 27], replicated
- mix_in_grad: float32 [192, 192], replicated
- bias_grad: float32 [192], replicated
- mix_out_grad: float32 [192, 192], replicated
All inputs are finite; a program needn't handle non-finite values.
Results may differ from a plain program's by a relative error of at most 0.008.
Values may be sent and summed in bfloat16 or wider, within the bound.
A program may use at most 64 MiB of HBM per device.

v0:
```python
import math

import jax
import jax.numpy as jnp
from jax import lax
from jax.sharding import PartitionSpec as P

INV_SQRT2 = 0.7071067811865476
INV_SQRT2PI = 0.3989422804014327


def extended(cells, sides, width):
    for axis, dim in sides:
        count = lax.axis_size(axis)
        ends = count - 1
        head = lax.slice_in_dim(cells, 0, width, axis=dim)
        tail = lax.slice_in_dim(cells, cells.shape[dim] - width, cells.shape[dim], axis=dim)
        cells = jnp.concatenate(
            [
                lax.ppermute(tail, axis, [(i, (i + 1) % count) for i in range(ends)]),
                cells,
                lax.ppermute(head, axis, [((i + 1) % count, i) for i in range(ends)]),
            ],
            axis=dim,
        )
    return cells


def tap_list():
    listing = []
    for plane_step in (-1, 0, 1):
        for row_step in (-1, 0, 1):
            for col_step in (-1, 0, 1):
                tap_index = 9 * (plane_step + 1) + 3 * (row_step + 1) + (col_step + 1)
                listing.append((tap_index, plane_step, row_step, col_step))
    return listing


def window(padded, plane_step, row_step, col_step, sign):
    planes = padded.shape[-3] - 2
    rows = padded.shape[-2] - 2
    cols = padded.shape[-1] - 2
    start_p = 1 + sign * plane_step
    start_r = 1 + sign * row_step
    start_c = 1 + sign * col_step
    return padded[
        ..., start_p : start_p + planes, start_r : start_r + rows, start_c : start_c + cols
    ]


def stencil(padded, kernel, sign):
    total = None
    for tap_index, plane_step, row_step, col_step in tap_list():
        piece = window(padded, plane_step, row_step, col_step, sign)
        weight = kernel[:, tap_index].reshape(kernel.shape[0], 1, 1, 1)
        term = weight * piece.astype(jnp.float32)
        total = term if total is None else total + term
    return total


def pad_planes(field):
    return jnp.pad(field, ((0, 0), (0, 0), (1, 1), (0, 0), (0, 0)))


def gelu_parts(pre):
    cdf = 0.5 * (1.0 + lax.erf(pre * INV_SQRT2))
    dens = jnp.exp(-0.5 * pre * pre) * INV_SQRT2PI
    return (cdf, cdf + pre * dens)


def chain(hidden, grad_out, mix_in, mix_bias, mix_out):
    pre = jnp.einsum("oc,bczxy->bozxy", mix_in, hidden, preferred_element_type=jnp.float32)
    pre = pre + mix_bias.reshape(-1, 1, 1, 1)
    cdf, slope = gelu_parts(pre)
    act = (pre * cdf).astype(jnp.bfloat16)
    act_grad = jnp.einsum("oc,bozxy->bczxy", mix_out, grad_out, preferred_element_type=jnp.float32)
    pre_grad = (act_grad * slope).astype(jnp.bfloat16)
    hidden_grad = jnp.einsum(
        "oc,bozxy->bczxy", mix_in, pre_grad, preferred_element_type=jnp.float32
    )
    return (act, pre_grad, hidden_grad.astype(jnp.bfloat16))


def per_device(inputs, cotangent, depth_kernel, mix_in, mix_bias, mix_out):
    rimmed = extended(inputs, (("sx", 3), ("sy", 4)), 1)
    padded = pad_planes(rimmed)
    hidden = stencil(padded, depth_kernel, 1).astype(jnp.bfloat16)
    act, pre_grad, hidden_grad = chain(hidden, cotangent, mix_in, mix_bias, mix_out)
    grad_rimmed = extended(hidden_grad, (("sx", 3), ("sy", 4)), 1)
    spread = stencil(pad_planes(grad_rimmed), depth_kernel, -1)
    input_grad = (cotangent.astype(jnp.float32) + spread).astype(jnp.bfloat16)
    out_sum = jnp.einsum("bozxy,bczxy->oc", cotangent, act, preferred_element_type=jnp.float32)
    bias_sum = jnp.sum(pre_grad.astype(jnp.float32), axis=(0, 2, 3, 4))
    in_sum = jnp.einsum("bozxy,bczxy->oc", pre_grad, hidden, preferred_element_type=jnp.float32)
    hidden_gf = hidden_grad.astype(jnp.float32)
    columns = [None] * 27
    for tap_index, plane_step, row_step, col_step in tap_list():
        piece = window(padded, plane_step, row_step, col_step, 1).astype(jnp.float32)
        columns[tap_index] = jnp.sum(hidden_gf * piece, axis=(0, 2, 3, 4))
    kern_sum = jnp.stack(columns, axis=1)
    kern_total, in_total, bias_total, out_total = lax.psum(
        (kern_sum, in_sum, bias_sum, out_sum), ("sx", "sy", "sample")
    )
    cells = inputs.shape[0] * inputs.shape[2] * inputs.shape[3] * inputs.shape[4]
    cells = cells * lax.axis_size("sx") * lax.axis_size("sy") * lax.axis_size("sample")
    factor = 1.0 / math.sqrt(cells)
    return (
        input_grad,
        kern_total * factor,
        in_total * factor,
        bias_total * factor,
        out_total * factor,
    )


def solution(mesh):
    placed = (
        P("sample", None, None, "sx", "sy"),
        P("sample", None, None, "sx", "sy"),
        P(),
        P(),
        P(),
        P(),
    )
    return jax.shard_map(
        per_device,
        mesh=mesh,
        in_specs=placed,
        out_specs=(P("sample", None, None, "sx", "sy"), P(), P(), P(), P()),
        check_vma=False,
    )
```

profile of v0, /device:TPU:1, one launch (start us, length us, event | category | flops | bytes accessed | tf_op | source)
XLA Modules:
  0.0 356.8 jit_solution(6085999447036030158)
XLA Ops:
  9.4 4.9 %collective-permute-start = (bf16[1,192,2,1,128]{4,1,3,2,0:T(8,128)(2,1)S(1)}, bf16[1,192,2,1,128]{4,1,3,2,0:T(8,128)(2,1)S(1)}, u32[]{:S(2)}, u32[]{:S(2)}) collective-permute-start(bf16[1,192,2,1,128]{4,1,3,2,0:T(8,128)(2,1)S(1)} %get-tuple-element.59), channel_id=1, source_target_pairs={{0,16},{16,32},{32,48},{48,64},{64,80},{80,96},{96,112},{1,17},{17... | collective-permute-start | bytes 294920 | tf_op jit(solution)/shard_map/ppermute | solution.py:20
  17.7 2.6 collective-permute-done.1
  21.0 2.5 fusion.121
  23.4 2.6 copy.33
  26.0 2.6 copy.34
  29.9 4.6 %collective-permute-start.2 = (bf16[1,192,2,18,1]{1,2,4,3,0:T(2,128)(2,1)}, bf16[1,192,2,18,1]{1,2,4,3,0:T(2,128)(2,1)}, u32[]{:S(2)}, u32[]{:S(2)}) collective-permute-start(bf16[1,192,2,18,1]{1,2,4,3,0:T(2,128)(2,1)} %copy.33), channel_id=1, source_target_pairs={{0,2},{2,4},{4,6},{6,8},{8,10},{10,12},{12,14},{1,3},{3,5},{5,7},{... | collective-permute-start | bytes 41480 | tf_op jit(solution)/shard_map/ppermute | solution.py:20
  36.1 2.5 copy.35
  38.5 2.4 copy.36
  41.2 4.6 %fusion.8 = bf16[1,192,4,18,130]{4,1,3,2,0:T(8,128)(2,1)S(1)} fusion(bf16[1,192,2,18,1]{4,1,3,2,0:T(8,128)(2,1)} %copy.36, bf16[1,192,2,18,128]{4,1,3,2,0:T(8,128)(2,1)S(1)} %constant_dynamic-update-slice_fusion, bf16[1,192,2,18,1]{4,1,3,2,0:T(8,128)(2,1)} %copy.35), kind=kLoop, calls=%fused_computation.40 | loop fusion | flops 21565440 | bytes 5391360 | tf_op jit(solution)/shard_map/concatenate | solution.py:18
  46.1 17.0 %fusion.103 = bf16[192,2,16,128]{3,0,2,1:T(8,128)(2,1)S(1)} fusion(f32[192]{0:T(256)S(1)} %bitcast.189, f32[192]{0:T(256)S(1)} %bitcast.191, f32[192]{0:T(256)S(1)} %bitcast.141, f32[192]{0:T(256)S(1)} %bitcast.143, f32[192]{0:T(256)S(1)} %bitcast.145, f32[192]{0:T(256)S(1)} %bitcast.147, f32[192]{0:T(256)S(1)} %bitcast.149, f32[192]{0:T(256)S(1)} %bitcast.151, ...), kind=kLoop, calls=%fused_computation.185 | loop fusion | flops 82575360 | bytes 33471744 | tf_op jit(solution)/shard_map/reshape.35
  67.3 3.6 %convert_reduce_fusion = (f32[192]{0:T(256)}, bf16[1,192,2,16,128]{4,1,3,2,0:T(8,128)(2,1)}) fusion(f32[192]{0:T(256)S(1)} %copy-done.61, f32[2,16,128,192]{2,3,1,0:T(8,128)S(1)} %fusion.116, bf16[192,192]{1,0:T(8,128)(2,1)S(1)} %copy-done.60, bf16[192,2,16,128]{3,2,1,0:T(8,128)(2,1)S(1)} %bitcast.138), kind=kOutput, calls=%fused_computation.163 | convolution fusion | flops 312213312 | bytes 6366720 | tf_op jit(solution)/shard_map/oc,bozxy->bczxy/dot_general | solution.py:76
  70.9 29.3 %fusion.85 = (f32[192]{0:T(256)}, f32[192]{0:T(256)}, f32[192]{0:T(256)}, f32[192]{0:T(256)}, f32[192]{0:T(256)}, /*index=5*/f32[192]{0:T(256)}, f32[192]{0:T(25...) fusion(bf16[1,192,4,18,130]{4,1,3,2,0:T(8,128)(2,1)} %copy-done, ...), kind=kOutput, calls=%fused_computation.155 | convolution fusion | flops 346026624 | bytes 31544832 | tf_op jit(solution)/shard_map/oc,bozxy->bczxy/dot_general | solution.py:78
  100.3 3.1 fusion.105
  104.1 2.4 collective-permute-start.4
  108.4 10.9 %fusion.76 = (f32[192]{0:T(256)}, f32[192]{0:T(256)}, f32[192]{0:T(256)}, f32[192]{0:T(256)}, f32[192]{0:T(256)}, /*index=5*/f32[192]{0:T(256)}, f32[192]{0:T(256)}, f32[192]{0:T(256)}, f32[192]{0:T(256)}) fusion(bf16[1,192,2,16,128]{4,1,3,2,0:T(8,128)(2,1)S(1)} %get-tuple-element.88, bf16[1,192,2,18,1]{4,1,3,2,0:T(8,128)(2,1)} %copy.36, ...), kind=kLoop, calls=%fused_computation.146 | loop fusion | flops 40892736 | bytes 6719232 | tf_op jit(solution)/shard_map/reduce_sum | solution.py:99
  119.3 2.9 stack.111
  122.2 68.7 %all-reduce.2 = (f32[192,27]{0,1:T(8,128)S(1)}, f32[192]{0:T(256)}) all-reduce(f32[192,27]{0,1:T(8,128)S(1)} %stack.111, f32[192]{0:T(256)} %get-tuple-element.89), channel_id=1, replica_groups=mesh['sx'=8,'sy'=8,'sample'=2] {'sx','sy','sample'}, use_global_device_ids=true, to_apply=%region_27.28 | all-reduce | flops 5376 | bytes 43008 | tf_op jit(solution)/shard_map/psum | solution.py:101
  194.6 2.6 copy.43
  200.1 4.6 %collective-permute-start.6 = (bf16[1,192,2,18,1]{1,2,4,3,0:T(2,128)(2,1)}, bf16[1,192,2,18,1]{1,2,4,3,0:T(2,128)(2,1)}, u32[]{:S(2)}, u32[]{:S(2)}) collective-permute-start(bf16[1,192,2,18,1]{1,2,4,3,0:T(2,128)(2,1)} %copy.43), channel_id=1, source_target_pairs={{0,2},{2,4},{4,6},{6,8},{8,10},{10,12},{12,14},{1,3},{3,5},{5,7},{... | collective-permute-start | bytes 41480 | tf_op jit(solution)/shard_map/ppermute | solution.py:20
  207.9 2.4 copy.46
  210.3 4.9 %select_maximum_fusion = bf16[1,192,4,18,130]{4,1,3,2,0:T(8,128)(2,1)S(1)} fusion(bf16[1,192,2,18,1]{4,1,3,2,0:T(8,128)(2,1)} %copy.46, bf16[1,192,2,18,1]{4,1,3,2,0:T(8,128)(2,1)S(1)} %copy.45, bf16[1,192,2,1,128]{4,1,3,2,0:T(8,128)(2,1)} %collective-permute-done.5, bf16[1,192,2,16,128]{4,1,3,2,0:T(8,128)(2,1)S(1)} %get-tuple-element.88, ...), kind=kLoop, calls=%fused_computation.31 | loop fusion | flops 32348160 | bytes 5391360 | tf_op jit(solution)/shard_map/concatenate | solution.py:18
  215.5 4.3 %pad_maximum_fusion = (bf16[1,192,2,18,129]{4,1,3,2,0:T(8,128)(2,1)S(1)}, bf16[1,192,2,18,129]{4,1,3,2,0:T(8,128)(2,1)S(1)}) fusion(bf16[1,192,2,18,1]{4,1,3,2,0:T(8,128)(2,1)S(1)} %copy-done.4, bf16[1,192,2,1,128]{4,1,3,2,0:T(8,128)(2,1)} %collective-permute-done.5, bf16[1,192,2,16,128]{4,1,3,2,0:T(8,128)(2,1)S(1)} %get-tuple-element.88, ...), kind=kLoop, calls=%fused_computation.79 | loop fusion | flops 14266368 | bytes 5363712 | tf_op jit(solution)/shard_map/concatenate | solution.py:18
  220.0 15.2 %fusion.90 = bf16[1,192,2,16,128]{4,1,3,2,0:T(8,128)(2,1)S(1)} fusion(bf16[1,192,2,16,128]{4,1,3,2,0:T(8,128)(2,1)S(1)} %get-tuple-element.88, bf16[1,192,4,18,130]{4,1,3,2,0:T(8,128)(2,1)S(1)} %select_maximum_fusion, bf16[1,192,2,18,129]{4,1,3,2,0:T(8,128)(2,1)S(1)} %get-tuple-element.52, bf16[1,192,2,1,128]{4,1,3,2,0:T(8,128)(2,1)S(1)} %collective-permute-done.4, ...), kind=kLoop, calls=%fused_computation.164 | loop fusion | flops 66846720 | bytes 42684672 | tf_op jit(solution)/shard_map/convert_element_type | solution.py:91
  237.3 110.9 %all-reduce.6.cloned.1.call-done = (f32[192,192]{1,0:T(8,128)}, f32[192,192]{1,0:T(8,128)}) async-done(((f32[192,192]{1,0:T(8,128)}, f32[192,192]{1,0:T(8,128)}), (f32[192,192]{1,0:T(8,128)}, f32[192,192]{1,0:T(8,128)})) %all-reduce.6.cloned.1.call-update) | async-done | bytes 294928 | tf_op jit(solution)/shard_map/psum | solution.py:101
  (155 shorter events, 29.6 us)
Async XLA Ops:
  7.2 55.9 %copy-start = (bf16[192,192]{1,0:T(8,128)(2,1)S(1)}, bf16[192,192]{1,0:T(8,128)(2,1)}, u32[]{:S(2)}) copy-start(bf16[192,192]{1,0:T(8,128)(2,1)} %param.9) | copy-start | bytes 221188
  7.2 9.1 %copy-start.13 = (f32[192,27]{0,1:T(8,128)S(1)}, f32[192,27]{0,1:T(8,128)}, u32[]{:S(2)}) copy-start(f32[192,27]{0,1:T(8,128)} %param.8) | copy-start | bytes 62212
  7.2 341.0 %all-reduce.6.cloned.1.call-start = ((), (), s32[]{:S(2)}) async-start(), calls=%async_computation | async-start | bytes 786432 | tf_op jit(solution)/shard_map/psum | solution.py:101
  7.2 9.8 %copy-start.6 = (bf16[1,192,2,16,128]{4,3,2,1,0:T(8,128)(2,1)S(1)}, bf16[1,192,2,16,128]{4,3,2,1,0:T(8,128)(2,1)}, u32[]{:S(2)}) copy-start(bf16[1,192,2,16,128]{4,3,2,1,0:T(8,128)(2,1)} %param.6) | copy-start | bytes 4718596
  9.4 36.4 %copy-start.5 = (bf16[1,192,2,16,128]{4,1,3,2,0:T(8,128)(2,1)}, bf16[1,192,2,16,128]{4,1,3,2,0:T(8,128)(2,1)S(1)}, u32[]{:S(2)}) copy-start(bf16[1,192,2,16,128]{4,1,3,2,0:T(8,128)(2,1)S(1)} %copy.30) | copy-start | bytes 4718596
  9.4 7.5 %collective-permute-start = (bf16[1,192,2,1,128]{4,1,3,2,0:T(8,128)(2,1)S(1)}, bf16[1,192,2,1,128]{4,1,3,2,0:T(8,128)(2,1)S(1)}, u32[]{:S(2)}, u32[]{:S(2)}) collective-permute-start(bf16[1,192,2,1,128]{4,1,3,2,0:T(8,128)(2,1)S(1)} %get-tuple-element.59), channel_id=1, source_target_pairs={{0,16},{16,32},{32,48},{48,64},{64,80},{80,96},{96,112},{1,17},{17... | collective-permute-start | bytes 294920 | tf_op jit(solution)/shard_map/ppermute | solution.py:20
  14.4 5.9 %collective-permute-start.1 = (bf16[1,192,2,1,128]{4,1,3,2,0:T(8,128)(2,1)S(1)}, bf16[1,192,2,1,128]{4,1,3,2,0:T(8,128)(2,1)S(1)}, u32[]{:S(2)}, u32[]{:S(2)}) collective-permute-start(bf16[1,192,2,1,128]{4,1,3,2,0:T(8,128)(2,1)S(1)} %get-tuple-element.60), channel_id=1, source_target_pairs={{16,0},{32,16},{48,32},{64,48},{80,64},{96,80},{112,96},{17,1},{33... | collective-permute-start | bytes 294920 | tf_op jit(solution)/shard_map/ppermute | solution.py:22
  17.0 28.9 %copy-start.10 = (bf16[1,192,2,1,128]{4,1,3,2,0:T(8,128)(2,1)}, bf16[1,192,2,1,128]{4,1,3,2,0:T(8,128)(2,1)S(1)}, u32[]{:S(2)}) copy-start(bf16[1,192,2,1,128]{4,1,3,2,0:T(8,128)(2,1)S(1)} %collective-permute-done) | copy-start | bytes 294916
  28.6 9.9 %collective-permute-start.3 = (bf16[1,192,2,18,1]{1,2,4,3,0:T(2,128)(2,1)}, bf16[1,192,2,18,1]{1,2,4,3,0:T(2,128)(2,1)}, u32[]{:S(2)}, u32[]{:S(2)}) collective-permute-start(bf16[1,192,2,18,1]{1,2,4,3,0:T(2,128)(2,1)} %copy.34), channel_id=1, source_target_pairs={{2,0},{4,2},{6,4},{8,6},{10,8},{12,10},{14,12},{3,1},{5,3},{7,5},{... | collective-permute-start | bytes 41480 | tf_op jit(solution)/shard_map/ppermute | solution.py:22
  29.9 6.1 %collective-permute-start.2 = (bf16[1,192,2,18,1]{1,2,4,3,0:T(2,128)(2,1)}, bf16[1,192,2,18,1]{1,2,4,3,0:T(2,128)(2,1)}, u32[]{:S(2)}, u32[]{:S(2)}) collective-permute-start(bf16[1,192,2,18,1]{1,2,4,3,0:T(2,128)(2,1)} %copy.33), channel_id=1, source_target_pairs={{0,2},{2,4},{4,6},{6,8},{8,10},{10,12},{12,14},{1,3},{3,5},{5,7},{... | collective-permute-start | bytes 41480 | tf_op jit(solution)/shard_map/ppermute | solution.py:20
  41.0 4.9 %copy-start.16 = (f32[192,1]{0,1:T(1,128)S(1)}, f32[192,1]{0,1:T(1,128)}, u32[]{:S(2)}) copy-start(f32[192,1]{0,1:T(1,128)} %get-tuple-element.66) | copy-start | bytes 2308
  41.0 4.9 %copy-start.18 = (f32[192,1]{0,1:T(1,128)S(1)}, f32[192,1]{0,1:T(1,128)}, u32[]{:S(2)}) copy-start(f32[192,1]{0,1:T(1,128)} %get-tuple-element.67) | copy-start | bytes 2308
  41.0 4.9 %copy-start.20 = (f32[192,1]{0,1:T(1,128)S(1)}, f32[192,1]{0,1:T(1,128)}, u32[]{:S(2)}) copy-start(f32[192,1]{0,1:T(1,128)} %get-tuple-element.68) | copy-start | bytes 2308
  41.0 4.9 %copy-start.22 = (f32[192,1]{0,1:T(1,128)S(1)}, f32[192,1]{0,1:T(1,128)}, u32[]{:S(2)}) copy-start(f32[192,1]{0,1:T(1,128)} %get-tuple-element.69) | copy-start | bytes 2308
  41.0 4.9 %copy-start.24 = (f32[192,1]{0,1:T(1,128)S(1)}, f32[192,1]{0,1:T(1,128)}, u32[]{:S(2)}) copy-start(f32[192,1]{0,1:T(1,128)} %get-tuple-element.70) | copy-start | bytes 2308
  41.0 4.9 %copy-start.26 = (f32[192,1]{0,1:T(1,128)S(1)}, f32[192,1]{0,1:T(1,128)}, u32[]{:S(2)}) copy-start(f32[192,1]{0,1:T(1,128)} %get-tuple-element.71) | copy-start | bytes 2308
  41.0 4.9 %copy-start.28 = (f32[192,1]{0,1:T(1,128)S(1)}, f32[192,1]{0,1:T(1,128)}, u32[]{:S(2)}) copy-start(f32[192,1]{0,1:T(1,128)} %get-tuple-element.72) | copy-start | bytes 2308
  41.0 4.9 %copy-start.30 = (f32[192,1]{0,1:T(1,128)S(1)}, f32[192,1]{0,1:T(1,128)}, u32[]{:S(2)}) copy-start(f32[192,1]{0,1:T(1,128)} %get-tuple-element.73) | copy-start | bytes 2308
  45.8 17.3 %copy-start.1 = (bf16[1,192,4,18,130]{4,1,3,2,0:T(8,128)(2,1)}, bf16[1,192,4,18,130]{4,1,3,2,0:T(8,128)(2,1)S(1)}, u32[]{:S(2)}) copy-start(bf16[1,192,4,18,130]{4,1,3,2,0:T(8,128)(2,1)S(1)} %fusion.8) | copy-start | bytes 10782724
  104.1 87.5 %collective-permute-start.4 = (bf16[1,192,2,1,128]{4,1,3,2,0:T(8,128)(2,1)}, bf16[1,192,2,1,128]{4,1,3,2,0:T(8,128)(2,1)S(1)}, u32[]{:S(2)}, u32[]{:S(2)}) collective-permute-start(bf16[1,192,2,1,128]{4,1,3,2,0:T(8,128)(2,1)} %get-tuple-element.57), channel_id=1, source_target_pairs={{0,16},{16,32},{32,48},{48,64},{64,80},{80,96},{96,112},{1,17},{17... | collective-permute-start | bytes 294920 | tf_op jit(solution)/shard_map/ppermute | solution.py:20
  106.5 85.1 %collective-permute-start.5 = (bf16[1,192,2,1,128]{4,1,3,2,0:T(8,128)(2,1)}, bf16[1,192,2,1,128]{4,1,3,2,0:T(8,128)(2,1)}, u32[]{:S(2)}, u32[]{:S(2)}) collective-permute-start(bf16[1,192,2,1,128]{4,1,3,2,0:T(8,128)(2,1)} %get-tuple-element.58), channel_id=1, source_target_pairs={{16,0},{32,16},{48,32},{64,48},{80,64},{96,80},{112,96},{17,1},{33... | collective-permute-start | bytes 294920 | tf_op jit(solution)/shard_map/ppermute | solution.py:22
  198.8 9.1 %collective-permute-start.7 = (bf16[1,192,2,18,1]{1,2,4,3,0:T(2,128)(2,1)}, bf16[1,192,2,18,1]{1,2,4,3,0:T(2,128)(2,1)}, u32[]{:S(2)}, u32[]{:S(2)}) collective-permute-start(bf16[1,192,2,18,1]{1,2,4,3,0:T(2,128)(2,1)} %copy.44), channel_id=1, source_target_pairs={{2,0},{4,2},{6,4},{8,6},{10,8},{12,10},{14,12},{3,1},{5,3},{7,5},{... | collective-permute-start | bytes 41480 | tf_op jit(solution)/shard_map/ppermute | solution.py:22
  200.1 5.9 %collective-permute-start.6 = (bf16[1,192,2,18,1]{1,2,4,3,0:T(2,128)(2,1)}, bf16[1,192,2,18,1]{1,2,4,3,0:T(2,128)(2,1)}, u32[]{:S(2)}, u32[]{:S(2)}) collective-permute-start(bf16[1,192,2,18,1]{1,2,4,3,0:T(2,128)(2,1)} %copy.43), channel_id=1, source_target_pairs={{0,2},{2,4},{4,6},{6,8},{8,10},{10,12},{12,14},{1,3},{3,5},{5,7},{... | collective-permute-start | bytes 41480 | tf_op jit(solution)/shard_map/ppermute | solution.py:20
  210.3 4.9 %copy-start.4 = (bf16[1,192,2,18,1]{4,1,3,2,0:T(8,128)(2,1)S(1)}, bf16[1,192,2,18,1]{4,1,3,2,0:T(8,128)(2,1)}, u32[]{:S(2)}) copy-start(bf16[1,192,2,18,1]{4,1,3,2,0:T(8,128)(2,1)} %copy.46) | copy-start | bytes 41476
  (47 other events, 207.6 us)
Sparse Core Ops, SparseCore 0:
  206.0 142.1 all-reduce.5
where the time goes:
time: 358 us; the launch traced here: 357 us
  waiting for transfers between devices  113 us (32%)
  blocking collectives  68.7 us (19%)
  other arithmetic  61.6 us (17%)
  matrix products  38.9 us (11%)
  local copies, waits for them, and re-layouts  36.1 us (10%)
  starting transfers between devices  22.9 us (6%)
  between operations  15.1 us (4%)
    psum x1, waiting for transfers between devices, per_device(): lax.psum((kern_sum, in_sum, bias_sum, out_sum), ('sx', 'sy', 'sample'))  111 us
    psum x1, blocking collectives, per_device(): lax.psum((kern_sum, in_sum, bias_sum, out_sum), ('sx', 'sy', 'sample'))  68.7 us
    dot_general x1, matrix products, chain(): jnp.einsum('oc,bozxy->bczxy', mix_in, pre_grad, preferred_element_type=jn...  29.3 us
    another operation x1, other arithmetic  17 us
    ppermute x4, starting transfers between devices, extended(): lax.ppermute(tail, axis, [(i, (i + 1) % count) for i in range(ends)])  16.5 us
    convert_element_type x1, other arithmetic, per_device(): input_grad = (cotangent.astype(jnp.float32) + spread).astype(jnp.bfloat16)  15.2 us
    concatenate x4, other arithmetic, extended(): jnp.concatenate([lax.ppermute(tail, axis, [(i, (i + 1) % count) for i in...  14.9 us
    reduce_sum x1, other arithmetic, per_device(): columns[tap_index] = jnp.sum(hidden_gf * piece, axis=(0, 2, 3, 4))  10.9 us
  transfers between devices with their start and end apart: 9, of which 2 were waited for; matrix products, arithmetic and copies ran while one was open for 15% of the time, Pallas kernels for 0%

commit v1 on v0

v1 whole, which is shorter than its diff:
```python
import functools
import math

import jax
import jax.numpy as jnp
from jax import lax
from jax.experimental import pallas as pl
from jax.experimental.pallas import tpu as pltpu
from jax.sharding import PartitionSpec as P

INV_SQRT2 = 0.7071067811865476
INV_SQRT2PI = 0.3989422804014327
MESH = pl.DeviceIdType.MESH
F32 = jnp.float32
BF16 = jnp.bfloat16

CH = 192
NR = 16
NC = 128
RR = NR + 2
BLK = 8
CHUNK = 48


def dot(a, b):
    return jnp.dot(a, b, preferred_element_type=F32)


def dot_nt(a, b):
    return lax.dot_general(a, b, (((1,), (1,)), ((), ())), preferred_element_type=F32)


def iota(shape, dim):
    return lax.broadcasted_iota(jnp.int32, shape, dim)


def one_hot(cond):
    return jnp.where(cond, 1.0, 0.0).astype(BF16)


def pack_matrix(i):
    k = iota((2 * NC, 128), 0)
    lane = iota((2 * NC, 128), 1)
    z = k // NC
    j = k - z * NC
    at = z * RR + i + 1
    return one_hot(((j == NC - 1) & (lane == at)) | ((j == 0) & (lane == 64 + at)))


def rim_matrix(at):
    lane = iota((128, 2 * NC), 0)
    j = iota((128, 2 * NC), 1)
    return one_hot(((j == 0) & (lane == at)) | ((j == 2 * NC - 1) & (lane == 64 + at)))


def shift_matrix():
    k = iota((NC, 2 * NC), 0)
    j = iota((NC, 2 * NC), 1)
    return one_hot(((j < NC) & (k == j - 1)) | ((j >= NC) & (k == j - NC + 1)))


def stencil_block(a0, am, ap, w, flip, rows, emit):
    k0 = [w[8 - t if flip else t, rows, :] for t in range(9)]
    kp = [w[18 + 8 - t if flip else 9 + t, rows, :] for t in range(9)]
    km = [w[9 + 8 - t if flip else 18 + t, rows, :] for t in range(9)]
    live = {}
    for r in range(RR):
        lower = [ref[r, 0, rows, :] for ref in (am, a0, ap)]
        upper = [ref[r, 1, rows, :] for ref in (am, a0, ap)]
        both = [u + v for u, v in zip(lower, upper)]
        for q in (1, 0, -1):
            i = r - 1 - q
            if not 0 <= i < NR:
                continue
            total = live.get(i, [None, None, None])
            for s in range(3):
                t = 3 * (q + 1) + s
                terms = (k0[t] * both[s], kp[t] * upper[s], km[t] * lower[s])
                total = [b if a is None else a + b for a, b in zip(total, terms)]
            live[i] = total
        if r >= 2:
            shared, first, second = live.pop(r - 2)
            emit(r - 2, shared + first, shared + second)


def tap_sums_block(g0, a0, am, ap, rows):
    sums = [[None] * 9 for _ in range(3)]
    grads = {}
    for r in range(RR):
        lower = [ref[r, 0, rows, :] for ref in (am, a0, ap)]
        upper = [ref[r, 1, rows, :] for ref in (am, a0, ap)]
        both = [u + v for u, v in zip(lower, upper)]
        if r < NR:
            first = g0[r + 1, 0, rows, :]
            second = g0[r + 1, 1, rows, :]
            grads[r] = (first + second, first, second)
        for q in (1, 0, -1):
            i = r - 1 - q
            if not 0 <= i < NR:
                continue
            shared, first, second = grads[i]
            for s in range(3):
                t = 3 * (q + 1) + s
                terms = (shared * both[s], first * upper[s], second * lower[s])
                for kind in range(3):
                    old = sums[kind][t]
                    sums[kind][t] = terms[kind] if old is None else old + terms[kind]
    lane = iota((BLK, 128), 1)
    out = jnp.zeros((BLK, 128), F32)
    for t in range(9):
        middle = sums[0][t] - sums[1][t] - sums[2][t]
        for p, value in ((0, sums[2][t]), (1, middle), (2, sums[1][t])):
            out = jnp.where(lane == 9 * p + t, jnp.sum(value, axis=1, keepdims=True), out)
    return out


def kernel(
    sizes, factor, phases,
    x_ref, cot_ref, dk_ref, bias_ref, mi_ref, mo_ref,
    ig_ref, kg_ref, mig_ref, bg_ref, mog_ref,
    xf, cf, xb, hb, a0, am, ap, b0, bm, bp, cb, ag, hid, w, mit, mot, turn,
    px, ph, prx, prh, pacc, halo, moa, mia, ba, kc, gs, ar, br, fin, bs,
    hsend, hrecv, asend, arecv, bsend, brecv, csend, crecv,
):
    n_sx, n_sy, n_sample = sizes
    comm = n_sx > 1
    n_group = n_sy * n_sample
    sx, sy, sample = (lax.axis_index(a) for a in ("sx", "sy", "sample"))
    me = sy * n_sample + sample

    def at_group(g):
        return {"sx": sx, "sy": g // n_sample, "sample": g % n_sample}

    def around(dx, dy):
        return {
            "sx": lax.rem(sx + dx + n_sx, n_sx),
            "sy": lax.rem(sy + dy + n_sy, n_sy),
            "sample": sample,
        }

    if comm:
        barrier = pltpu.get_barrier_semaphore()
        for d in range(1, n_group):
            pl.semaphore_signal(barrier, inc=1, device_id=at_group(lax.rem(me + d, n_group)), device_id_type=MESH)
        for d in range(1, n_sx):
            pl.semaphore_signal(barrier, inc=1, device_id=around(d, 0), device_id_type=MESH)
        for dx in (-1, 1):
            for dy in (-1, 1):
                pl.semaphore_signal(barrier, inc=1, device_id=around(dx, dy), device_id_type=MESH)

    pack_to = ((0, 1, 0), (1, 1, 1), (-1, 1, 2), (0, -1, 3), (1, -1, 4), (-1, -1, 5))

    def pack_copy(which, src, dst, slot):
        dx, dy, at = pack_to[slot]
        return pltpu.make_async_remote_copy(
            src_ref=src, dst_ref=dst.at[at], send_sem=hsend.at[which, at], recv_sem=hrecv.at[which, at],
            device_id=around(dx, dy), device_id_type=MESH,
        )

    def slab_copy(which, ref, up):
        return pltpu.make_async_remote_copy(
            src_ref=ref.at[NR if up else 1], dst_ref=ref.at[0 if up else NR + 1],
            send_sem=hsend.at[which, 6 + up], recv_sem=hrecv.at[which, 6 + up],
            device_id=around(1 if up else -1, 0), device_id_type=MESH,
        )

    def rim(recv):
        lane = iota((CH, 128), 1)
        left = lane < 64
        low = jnp.where(left, lane, lane - 64)

        def piece(slot, dx, dy):
            ok = (sx + dx >= 0) & (sx + dx < n_sx) & (sy + dy >= 0) & (sy + dy < n_sy)
            return jnp.where(ok, recv[slot].astype(F32), 0.0)

        mid = jnp.where(left, piece(0, 0, -1), piece(3, 0, 1))
        top = jnp.where(left, piece(1, -1, -1), piece(4, -1, 1))
        end = jnp.where(left, piece(2, 1, -1), piece(5, 1, 1))
        top = pltpu.roll(top, 128 - 16, axis=1)
        end = pltpu.roll(end, 16, axis=1)
        first = (low == 0) | (low == RR)
        last = (low == RR - 1) | (low == 2 * RR - 1)
        return jnp.where(first, top, jnp.where(last, end, mid)).astype(BF16)

    def spread(rows_ref, mid, back, ahead, r, z, edge):
        value = rows_ref[r, z]
        if edge:
            ok = sx > 0 if r == 0 else sx < n_sx - 1
            value = jnp.where(ok, value.astype(F32), 0.0).astype(BF16)
        mid[r, z] = value.astype(F32)
        lhs = jnp.concatenate([value, halo[...]], axis=1)
        rhs = jnp.concatenate([turn[...], rim_matrix(z * RR + r)], axis=0)
        both = dot(lhs, rhs)
        back[r, z] = both[:, :NC]
        ahead[r, z] = both[:, NC:]

    def spread_all(which, rows_ref, mid, back, ahead, sent, recv):
        if comm:
            for slot in range(6):
                pack_copy(which, sent, recv, slot).wait_recv()
            halo[...] = rim(recv)
        else:
            halo[...] = jnp.zeros_like(halo)

        @pl.loop(1, NR + 1)
        def _(r):
            for z in range(2):
                spread(rows_ref, mid, back, ahead, r, z, False)

        if comm:
            slab_copy(which, rows_ref, 0).wait_recv()
            slab_copy(which, rows_ref, 1).wait_recv()
        else:
            rows_ref[0] = jnp.zeros_like(rows_ref[0])
            rows_ref[NR + 1] = jnp.zeros_like(rows_ref[0])
        for r in (0, NR + 1):
            for z in range(2):
                spread(rows_ref, mid, back, ahead, r, z, True)
        if comm:
            for slot in range(6):
                pack_copy(which, sent, recv, slot).wait_send()
            slab_copy(which, rows_ref, 0).wait_send()
            slab_copy(which, rows_ref, 1).wait_send()

    @pl.loop(0, 24)
    def _(k):
        at = pl.ds(pl.multiple_of(k * 256, 256), 256)
        xf[at, :] = x_ref[at, :].astype(F32)

    pacc[...] = jnp.zeros_like(pacc)

    @pl.loop(0, NR)
    def _(i):
        for z in range(2):
            xb[i + 1, z] = xf[pl.ds(z * NR + i, CH, stride=2 * NR), :].astype(BF16)
        pacc[...] += dot(jnp.concatenate([xb[i + 1, 0], xb[i + 1, 1]], axis=1), pack_matrix(i))

    px[...] = pacc[...].astype(BF16)
    if comm:
        pl.semaphore_wait(barrier, n_group - 1 + n_sx - 1 + 4)
        for slot in range(6):
            pack_copy(0, px, prx, slot).start()
        slab_copy(0, xb, 0).start()
        slab_copy(0, xb, 1).start()

    turn[...] = shift_matrix()
    eye = one_hot(iota((CH, CH), 0) == iota((CH, CH), 1))
    mit[...] = dot_nt(eye, mi_ref[...]).astype(BF16)
    mot[...] = dot_nt(eye, mo_ref[...]).astype(BF16)
    tall = jnp.concatenate([dk_ref[...], bias_ref[...], jnp.zeros((100, CH), F32)], axis=0)
    tall = jnp.concatenate([tall, jnp.zeros((128, 64), F32)], axis=1)
    kc[...] = tall.T[:CH]

    @pl.loop(0, CH // BLK)
    def _(b):
        rows = pl.ds(pl.multiple_of(b * BLK, BLK), BLK)
        value = kc[rows, :]
        wide = [jnp.broadcast_to(value[:, k : k + 1], (BLK, 128)) for k in range(28)]
        for t in range(9):
            w[t, rows, :] = wide[9 + t]
            w[9 + t, rows, :] = wide[18 + t] - wide[9 + t]
            w[18 + t, rows, :] = wide[t] - wide[9 + t]
        w[27, rows, :] = wide[27]

    @pl.loop(0, 24)
    def _(k):
        at = pl.ds(pl.multiple_of(k * 256, 256), 256)
        cf[at, :] = cot_ref[at, :].astype(F32)

    @pl.loop(0, NR)
    def _(i):
        value = jnp.concatenate([cf[pl.ds(z * NR + i, CH, stride=2 * NR), :] for z in range(2)], axis=1).astype(BF16)
        cb[i] = value
        ag[i] = dot(mot[...], value)

    spread_all(0, xb, a0, am, ap, px, prx)

    if phases >= 1:
        @pl.loop(0, CH // BLK)
        def _(b):
            rows = pl.ds(pl.multiple_of(b * BLK, BLK), BLK)

            def emit(i, first, second):
                hid[i, rows, 0:NC] = first
                hid[i, rows, NC : 2 * NC] = second

            stencil_block(a0, am, ap, w, False, rows, emit)

    pacc[...] = jnp.zeros_like(pacc)
    moa[...] = jnp.zeros_like(moa)
    mia[...] = jnp.zeros_like(mia)
    ba[...] = jnp.zeros_like(ba)

    if phases >= 2:
        @pl.loop(0, NR)
        def _(i):
            hidden = hid[i].astype(BF16)
            shift = w[27]
            pre = dot(mi_ref[...], hidden) + jnp.concatenate([shift, shift], axis=1)
            cdf = 0.5 * (1.0 + lax.erf(pre * INV_SQRT2))
            dens = jnp.exp(-0.5 * pre * pre) * INV_SQRT2PI
            act = (pre * cdf).astype(BF16)
            pg = (ag[i] * (cdf + pre * dens)).astype(BF16)
            moa[...] += dot_nt(cb[i], act)
            mia[...] += dot_nt(pg, hidden)
            ba[...] += dot_nt(jnp.ones((8, 2 * NC), BF16), pg)
            hg = dot(mit[...], pg).astype(BF16)
            hb[i + 1, 0] = hg[:, :NC]
            hb[i + 1, 1] = hg[:, NC:]
            b0[i + 1, 0] = hg[:, :NC].astype(F32)
            b0[i + 1, 1] = hg[:, NC:].astype(F32)
            pacc[...] += dot(hg, pack_matrix(i))

    ph[...] = pacc[...].astype(BF16)
    if comm:
        for slot in range(6):
            pack_copy(1, ph, prh, slot).start()
        slab_copy(1, hb, 0).start()
        slab_copy(1, hb, 1).start()

    def scatter(g):
        return pltpu.make_async_remote_copy(
            src_ref=gs.at[g], dst_ref=ar.at[me], send_sem=asend.at[g], recv_sem=arecv.at[me],
            device_id=at_group(g), device_id_type=MESH,
        )

    for rg in range(4):
        at = pl.ds(rg * CHUNK, CHUNK)
        gs[rg] = moa[at, 0:128]
        gs[4 + rg] = jnp.concatenate([moa[at, 128:192], mia[at, 0:64]], axis=1)
        gs[8 + rg] = mia[at, 64:192]
    if comm:
        for d in range(1, n_group):
            g = lax.rem(me + d, n_group)

            @pl.when(g < 12)
            def _():
                scatter(g).start()

    if phases >= 3:
        @pl.loop(0, CH // BLK)
        def _(b):
            rows = pl.ds(pl.multiple_of(b * BLK, BLK), BLK)
            kc[rows, :] = tap_sums_block(b0, a0, am, ap, rows)

    flat = jnp.concatenate([kc[...], jnp.zeros((64, 128), F32)], axis=0).T[:32]
    whole = jnp.concatenate([ba[0:1], jnp.zeros((1, 64), F32)], axis=1)
    flat = jnp.where(iota((32, 256), 0) == 27, whole, flat)
    for g in (12, 13):
        gs[g, 0:32] = flat[:, 128 * (g - 12) : 128 * (g - 11)]
        gs[g, 32:48] = jnp.zeros((16, 128), F32)
    for g in (14, 15):
        gs[g] = jnp.zeros((CHUNK, 128), F32)
    if comm:
        for d in range(1, n_group):
            g = lax.rem(me + d, n_group)

            @pl.when(g >= 12)
            def _():
                scatter(g).start()

    spread_all(1, hb, b0, bm, bp, ph, prh)

    def input_grad(start, stop):
        @pl.loop(start, stop)
        def _(b):
            rows = pl.ds(pl.multiple_of(b * BLK, BLK), BLK)

            def emit(i, first, second):
                for z, value in ((0, first), (1, second)):
                    at = pl.ds(b * (BLK * 2 * NR) + z * NR + i, BLK, stride=2 * NR)
                    xf[at, :] = cf[at, :] + value

            stencil_block(b0, bm, bp, w, True, rows, emit)
            at = pl.ds(pl.multiple_of(b * 256, 256), 256)
            ig_ref[at, :] = xf[at, :].astype(BF16)

    def share(d):
        return pltpu.make_async_remote_copy(
            src_ref=bs, dst_ref=br.at[sx], send_sem=bsend.at[d], recv_sem=brecv.at[sx],
            device_id=around(d, 0), device_id_type=MESH,
        )

    def publish(g):
        return pltpu.make_async_remote_copy(
            src_ref=fin.at[me], dst_ref=fin.at[me], send_sem=csend.at[g], recv_sem=crecv.at[me],
            device_id=at_group(g), device_id_type=MESH,
        )

    def arrived(ref, sem, slot):
        pltpu.make_async_remote_copy(
            src_ref=ref.at[slot], dst_ref=ref.at[slot], send_sem=asend.at[0], recv_sem=sem.at[slot],
            device_id=around(1, 0), device_id_type=MESH,
        ).wait_recv()

    if phases >= 4:
        input_grad(0, 8)
    if comm:
        for d in range(1, n_group):
            arrived(ar, arecv, lax.rem(me + d, n_group))
        ar[me] = gs[me]
        total = ar[0]
        for g in range(1, n_group):
            total = total + ar[g]
        bs[...] = total
        for d in range(1, n_sx):
            share(d).start()
        br[sx] = total
    if phases >= 4:
        input_grad(8, 16)
    if comm:
        for d in range(1, n_sx):
            arrived(br, brecv, lax.rem(sx + d, n_sx))
        total = br[0]
        for k in range(1, n_sx):
            total = total + br[k]
        fin[me] = total * factor
        for d in range(1, n_group):
            publish(lax.rem(me + d, n_group)).start()
    if phases >= 4:
        input_grad(16, 24)
    if comm:
        for d in range(1, n_group):
            arrived(fin, crecv, lax.rem(me + d, n_group))
        for d in range(1, n_group):
            g = lax.rem(me + d, n_group)
            scatter(g).wait_send()
            publish(g).wait_send()
        for d in range(1, n_sx):
            share(d).wait_send()
    else:
        fin[...] = gs[...]

    for rg in range(4):
        at = pl.ds(rg * CHUNK, CHUNK)
        mog_ref[at, 0:128] = fin[rg]
        mog_ref[at, 128:192] = fin[4 + rg][:, 0:64]
        mig_ref[at, 0:64] = fin[4 + rg][:, 64:128]
        mig_ref[at, 64:192] = fin[8 + rg]
    kg_ref[:, 0:128] = fin[12][0:27]
    kg_ref[:, 128:192] = fin[13][0:27, 0:64]
    bg_ref[:, 0:128] = fin[12][27:28]
    bg_ref[:, 128:192] = fin[13][27:28, 0:64]


def per_device(sizes, factor, phases, inputs, cotangent, depth_kernel, mix_in, mix_bias, mix_out):
    flat = (CH * 2 * NR, NC)
    vm = pltpu.VMEM
    field = (RR, 2, CH, NC)
    dma = pltpu.SemaphoreType.DMA
    n_sx, n_sy, n_sample = sizes
    n_group = n_sy * n_sample
    scratch = [
        vm(flat, F32), vm(flat, F32),
        vm(field, BF16), vm(field, BF16),
        vm(field, F32), vm(field, F32), vm(field, F32),
        vm(field, F32), vm(field, F32), vm(field, F32),
        vm((NR, CH, 2 * NC), BF16), vm((NR, CH, 2 * NC), F32), vm((NR, CH, 2 * NC), F32),
        vm((28, CH, 128), F32),
        vm((CH, CH), BF16), vm((CH, CH), BF16), vm((NC, 2 * NC), BF16),
        vm((CH, 128), BF16), vm((CH, 128), BF16), vm((6, CH, 128), BF16), vm((6, CH, 128), BF16),
        vm((CH, 128), F32), vm((CH, 128), BF16),
        vm((CH, CH), F32), vm((CH, CH), F32), vm((8, CH), F32), vm((CH, 128), F32),
        vm((16, CHUNK, 128), F32), vm((16, CHUNK, 128), F32), vm((max(n_sx, 2), CHUNK, 128), F32),
        vm((16, CHUNK, 128), F32), vm((CHUNK, 128), F32),
        dma((2, 8)), dma((2, 8)), dma((16,)), dma((16,)), dma((8,)), dma((8,)), dma((16,)), dma((16,)),
    ]
    full = pl.BlockSpec(memory_space=pltpu.VMEM)
    params = dict(vmem_limit_bytes=63 * 1024 * 1024)
    if n_sx > 1:
        params.update(collective_id=0, has_side_effects=True)
    ig, kg, mig, bg, mog = pl.pallas_call(
        functools.partial(kernel, sizes, factor, phases),
        out_shape=(
            jax.ShapeDtypeStruct(flat, BF16),
            jax.ShapeDtypeStruct((27, CH), F32),
            jax.ShapeDtypeStruct((CH, CH), F32),
            jax.ShapeDtypeStruct((1, CH), F32),
            jax.ShapeDtypeStruct((CH, CH), F32),
        ),
        in_specs=[full] * 6,
        out_specs=(full,) * 5,
        scratch_shapes=scratch,
        compiler_params=pltpu.CompilerParams(**params),
        name="block",
    )(
        inputs.reshape(flat),
        cotangent.reshape(flat),
        depth_kernel.T,
        mix_bias.reshape(1, CH),
        mix_in,
        mix_out,
    )
    return (ig.reshape(inputs.shape), kg.T, mig, bg.reshape(CH), mog)


def solution(mesh, phases=9):
    sizes = tuple(mesh.shape[a] for a in ("sx", "sy", "sample"))
    cells = sizes[0] * sizes[1] * sizes[2] * 2 * NR * NC
    field = P("sample", None, None, "sx", "sy")
    return jax.shard_map(
        functools.partial(per_device, sizes, 1.0 / math.sqrt(cells), phases),
        mesh=mesh,
        in_specs=(field, field, P(), P(), P(), P()),
        out_specs=(field, P(), P(), P(), P()),
        check_vma=False,
    )
```

time: 358 us -> 72.1 us (0.20)
  waiting for transfers between devices: 113 us -> 0 us
  blocking collectives: 68.7 us -> 0 us
  Pallas kernels: 0 us -> 65.8 us
  other arithmetic: 61.6 us -> 0 us
  matrix products: 38.9 us -> 0 us
  local copies, waits for them, and re-layouts: 36.1 us -> 5.42 us
  starting transfers between devices: 22.9 us -> 0 us
  between operations: 15.1 us -> 0.68 us
    psum x1 -> x0, waiting for transfers between devices: 111 us -> none  [per_device(): lax.psum((kern_sum, in_sum, bias_sum, out_sum), ('sx', 'sy', 'sample'))]
    psum x1 -> x0, blocking collectives: 68.7 us -> none  [per_device(): lax.psum((kern_sum, in_sum, bias_sum, out_sum), ('sx', 'sy', 'sample'))]
    pallas_call x0 -> x1, Pallas kernels: none -> 65.8 us  [per_device(): pl.pallas_call(functools.partial(kernel, sizes, factor, phases), out_shap...]
    dot_general x5 -> x0, matrix products: 38.9 us -> none  [the longest x1 29.3 us: chain(): jnp.einsum('oc,bozxy->bczxy', mix_in, pre_grad, preferred_element_type=jn...]
    ppermute x8 -> x0, starting transfers between devices: 22.9 us -> none  [the longest x4 16.5 us: extended(): lax.ppermute(tail, axis, [(i, (i + 1) % count) for i in range(ends)])]
    another operation x1 -> x0, other arithmetic: 17 us -> none
    slice x10 -> x0, local copies, waits for them, and re-layouts: 16.7 us -> none  [the longest x6 10.3 us: extended(): lax.slice_in_dim(cells, cells.shape[dim] - width, cells.shape[dim], axis=...]
    convert_element_type x1 -> x0, other arithmetic: 15.2 us -> none  [per_device(): input_grad = (cotangent.astype(jnp.float32) + spread).astype(jnp.bfloat16)]
  transfers between devices with their start and end apart: 9 -> 0, of which waited for: 2 -> 0; matrix products, arithmetic and copies ran while one was open for 15% -> 0% of each run, Pallas kernels for 0% -> 0%
where the time goes in v1:
time: 72.1 us; the launch traced here: 71.9 us
  Pallas kernels  65.8 us (91%)
  local copies, waits for them, and re-layouts  5.42 us (8%)
    pallas_call x1, Pallas kernels, per_device(): pl.pallas_call(functools.partial(kernel, sizes, factor, phases), out_shap...  65.8 us
    unnamed x13, local copies, waits for them, and re-layouts  5.42 us

profile of v1, /device:TPU:1, one launch (start us, length us, event | category | flops | bytes accessed | tf_op | source)
XLA Modules:
  0.0 71.9 jit_solution(7567039958486507415)
XLA Ops:
  0.6 65.8 %block.1 = (bf16[6144,128]{1,0:T(8,128)(2,1)}, f32[27,192]{1,0:T(8,128)}, f32[192,192]{1,0:T(8,128)}, f32[1,192]{1,0:T(1,128)}, f32[192,192]{1,0:T(8,128)}) custom-call(bf16[6144,128]{1,0:T(8,128)(2,1)} %bitcast.7, bf16[6144,128]{1,0:T(8,128)(2,1)} %bitcast.8, f32[27,192]{1,0:T(8,128)} %bitcast.10, f32[1,192]{1,0:T(1,128)} %bitcast.12, ...), custom_call_target="tpu_custom_call" | custom-call | tf_op jit(solution)/shard_map/block/pallas_call | solution.py:472
  66.4 0.0 copy-start.2
  66.4 0.0 copy-start.1
  66.4 0.0 copy-start.3
  66.4 0.0 copy-start
  66.5 2.9 %copy.16 = bf16[1,192,2,16,128]{4,3,2,1,0:T(8,128)(2,1)} copy(bf16[1,192,2,16,128]{4,3,2,1,0:T(8,128)(2,1)} %bitcast.9) | data formatting | bytes 3145728
  69.3 0.0 copy-done.2
  69.3 0.6 copy.17
  69.9 0.0 copy-done.1
  69.9 0.7 copy.18
  70.6 0.0 copy-done.3
  70.6 0.6 copy.19
  71.2 0.0 copy-done
  71.2 0.7 copy.20
Async XLA Ops:
  66.4 2.9 %copy-start.2 = (f32[27,192]{1,0:T(8,128)S(1)}, f32[27,192]{1,0:T(8,128)}, u32[]{:S(2)}) copy-start(f32[27,192]{1,0:T(8,128)} %get-tuple-element.11) | copy-start | bytes 62212
  66.4 3.5 %copy-start.1 = (f32[192,192]{1,0:T(8,128)S(1)}, f32[192,192]{1,0:T(8,128)}, u32[]{:S(2)}) copy-start(f32[192,192]{1,0:T(8,128)} %get-tuple-element.22) | copy-start | bytes 442372
  66.4 4.2 %copy-start.3 = (f32[1,192]{1,0:T(1,128)S(1)}, f32[1,192]{1,0:T(1,128)}, u32[]{:S(2)}) copy-start(f32[1,192]{1,0:T(1,128)} %get-tuple-element.13) | copy-start | bytes 2308
  66.4 4.7 %copy-start = (f32[192,192]{1,0:T(8,128)S(1)}, f32[192,192]{1,0:T(8,128)}, u32[]{:S(2)}) copy-start(f32[192,192]{1,0:T(8,128)} %get-tuple-element.24) | copy-start | bytes 442372

commit v2 on v0

v2 whole, which is shorter than its diff:
```python
import functools
import math

import jax
import jax.numpy as jnp
from jax import lax
from jax.experimental import pallas as pl
from jax.experimental.pallas import tpu as pltpu
from jax.sharding import PartitionSpec as P

INV_SQRT2 = 0.7071067811865476
INV_SQRT2PI = 0.3989422804014327
MESH = pl.DeviceIdType.MESH
F32 = jnp.float32
BF16 = jnp.bfloat16

CH = 192
NR = 16
NC = 128
RR = NR + 2
BLK = 8
WIDE = 16
CHUNK = 48
MIXES = 12
CHUNKS = 14


def dot(a, b):
    return jnp.dot(a, b, preferred_element_type=F32)


def dot_nt(a, b):
    return lax.dot_general(a, b, (((1,), (1,)), ((), ())), preferred_element_type=F32)


def iota(shape, dim):
    return lax.broadcasted_iota(jnp.int32, shape, dim)


def one_hot(cond):
    return jnp.where(cond, 1.0, 0.0).astype(BF16)


def block_of(b, size):
    return pl.ds(pl.multiple_of(b * size, size), size)


def rim_place(r, z):
    if isinstance(r, int) and r == 0:
        return 64 + 2 * z
    if isinstance(r, int) and r == RR - 1:
        return 68 + 2 * z
    return 4 * (r - 1) + 2 * z


def pick_matrix():
    u = iota((8, 4 * NC), 0)
    k = iota((8, 4 * NC), 1)
    return one_hot(k == (u // 2) * NC + jnp.where(u % 2 == 0, NC - 1, 0))


def rim_matrix(at):
    lane = iota((128, 2 * NC), 0)
    j = iota((128, 2 * NC), 1)
    return one_hot(((j == 0) & (lane == at)) | ((j == 2 * NC - 1) & (lane == at + 1)))


def shift_matrix():
    k = iota((NC, 2 * NC), 0)
    j = iota((NC, 2 * NC), 1)
    return one_hot(((j < NC) & (k == j - 1)) | ((j >= NC) & (k == j - NC + 1)))


def swap_matrix():
    k = iota((256, 256), 0)
    j = iota((256, 256), 1)
    return one_hot((k // 16 == j % 16) & (k % 16 == j // 16))


def tap_matrix(d):
    row = iota((128, 256), 0)
    k = jnp.where(row < 96, row % 32, -2)
    t = 2 * d + jnp.where(iota((128, 256), 1) < 128, 0, 1)
    plus = jnp.where(t < 9, t + 9, jnp.where(t < 18, t + 9, jnp.where(t < 27, t - 18, 27)))
    minus = jnp.where((t < 9) | (t > 26), -1, jnp.where(t < 18, t, t - 9))
    return (jnp.where(k == plus, 1.0, 0.0) - jnp.where(k == minus, 1.0, 0.0)).astype(BF16)


def stencil_block(a0, am, ap, w, flip, rows, emit):
    k0 = [w[8 - t if flip else t, rows, :] for t in range(9)]
    kp = [w[18 + 8 - t if flip else 9 + t, rows, :] for t in range(9)]
    km = [w[9 + 8 - t if flip else 18 + t, rows, :] for t in range(9)]
    live = {}
    for r in range(RR):
        lower = [ref[r, 0, rows, :] for ref in (am, a0, ap)]
        upper = [ref[r, 1, rows, :] for ref in (am, a0, ap)]
        both = [u + v for u, v in zip(lower, upper)]
        for q in (1, 0, -1):
            i = r - 1 - q
            if not 0 <= i < NR:
                continue
            total = live.get(i, [None, None, None])
            for s in range(3):
                t = 3 * (q + 1) + s
                terms = (k0[t] * both[s], kp[t] * upper[s], km[t] * lower[s])
                total = [b if a is None else a + b for a, b in zip(total, terms)]
            live[i] = total
        if r >= 2:
            shared, first, second = live.pop(r - 2)
            emit(r - 2, shared + first, shared + second)


def tap_sums_block(g0, a0, am, ap, rows):
    def step(r, sums):
        sums = list(sums)
        first = g0[r + 1, 0, rows, :]
        second = g0[r + 1, 1, rows, :]
        shared = first + second
        for q in range(3):
            for s, ref in enumerate((am, a0, ap)):
                lower = ref[r + q, 0, rows, :]
                upper = ref[r + q, 1, rows, :]
                t = 3 * q + s
                sums[t] = sums[t] + shared * (lower + upper)
                sums[9 + t] = sums[9 + t] + first * upper
                sums[18 + t] = sums[18 + t] + second * lower
        return tuple(sums)

    sums = lax.fori_loop(0, NR, step, tuple(jnp.zeros((BLK, NC), F32) for _ in range(27)), unroll=8)
    middle = [sums[t] - sums[9 + t] - sums[18 + t] for t in range(9)]
    return list(sums[18:]) + middle + list(sums[9:18])


def kernel(
    sizes, factor,
    x_hbm, cot_hbm, dk_hbm, bias_hbm, mi_hbm, mo_hbm,
    ig_hbm, sums_ref,
    xv, cv, ov, dk, bias, mi, mo,
    xb, hb, a0, am, ap, b0, bm, bp, cb, ag, hid, w, acc, mit, mot, turn, swap,
    px, ph, prx, prh, edge, halo, moa, mia, tall, flat, gs, ar, br, fin, bs,
    load, save, hsend, hrecv, asend, arecv, bsend, brecv, csend, crecv,
):
    n_sx, n_sy, n_sample = sizes
    comm = n_sx > 1
    n_group = n_sy * n_sample
    sx, sy, sample = (lax.axis_index(a) for a in ("sx", "sy", "sample"))
    me = sy * n_sample + sample

    def at_group(g):
        return {"sx": sx, "sy": g // n_sample, "sample": g % n_sample}

    def around(dx, dy):
        return {
            "sx": lax.rem(sx + dx + n_sx, n_sx),
            "sy": lax.rem(sy + dy + n_sy, n_sy),
            "sample": sample,
        }

    third = CH // 3
    loads = [pltpu.make_async_copy(x_hbm.at[pl.ds(third * k, third)], xv.at[pl.ds(third * k, third)], load.at[k]) for k in range(3)]
    loads += [
        pltpu.make_async_copy(src, dst, load.at[3 + k])
        for k, (src, dst) in enumerate(((mi_hbm, mi), (mo_hbm, mo), (dk_hbm, dk), (bias_hbm, bias), (cot_hbm, cv)))
    ]
    with jax.named_scope("start"):
        for copy in loads:
            copy.start()
        if comm:
            barrier = pltpu.get_barrier_semaphore()
            for d in range(1, n_group):
                pl.semaphore_signal(barrier, inc=1, device_id=at_group(lax.rem(me + d, n_group)), device_id_type=MESH)
            for d in range(1, n_sx):
                pl.semaphore_signal(barrier, inc=1, device_id=around(d, 0), device_id_type=MESH)
            for dx in (-1, 1):
                for dy in (-1, 1):
                    pl.semaphore_signal(barrier, inc=1, device_id=around(dx, dy), device_id_type=MESH)

    pack_to = ((0, 1, 0), (1, 1, 1), (-1, 1, 2), (0, -1, 3), (1, -1, 4), (-1, -1, 5))

    def pack_copy(which, src, dst, slot):
        dx, dy, at = pack_to[slot]
        if dx:
            src, dst = src.at[3 if dx > 0 else 0], dst.at[at, 0]
        else:
            dst = dst.at[at]
        return pltpu.make_async_remote_copy(
            src_ref=src, dst_ref=dst, send_sem=hsend.at[which, at], recv_sem=hrecv.at[which, at],
            device_id=around(dx, dy), device_id_type=MESH,
        )

    def slab_copy(which, ref, up):
        return pltpu.make_async_remote_copy(
            src_ref=ref.at[NR if up else 1], dst_ref=ref.at[0 if up else NR + 1],
            send_sem=hsend.at[which, 6 + up], recv_sem=hrecv.at[which, 6 + up],
            device_id=around(1 if up else -1, 0), device_id_type=MESH,
        )

    def pack_edges(sent):
        for k in range(4):
            sent[k] = jnp.concatenate([edge[2 * k], edge[2 * k + 1]], axis=0).astype(BF16)

    def send_edges(which, sent, recv):
        if comm:
            for slot in range(6):
                pack_copy(which, sent, recv, slot).start()

    def rim(recv):
        def piece(slot, block, dx, dy):
            ok = (sx + dx >= 0) & (sx + dx < n_sx) & (sy + dy >= 0) & (sy + dy < n_sy)
            return jnp.where(ok, recv[slot, block].astype(F32), 0.0)

        row = iota((16, CH), 0)
        left = row % 2 == 0
        tall = [jnp.where(left, piece(0, k, 0, -1), piece(3, k, 0, 1)) for k in range(4)]
        top = jnp.where(left, piece(1, 0, -1, -1), piece(4, 0, -1, 1))[8:16]
        end = jnp.where(left, piece(2, 0, 1, -1), piece(5, 0, 1, 1))[0:8]
        tall.append(pltpu.roll(jnp.where(row[0:8] >= 4, top, end), 4, axis=0))
        tall.append(jnp.zeros((128 - 72, CH), F32))
        square = jnp.concatenate(tall, axis=0)
        square = jnp.concatenate([square, jnp.zeros((128, 64), F32)], axis=1)
        return square.T[:CH].astype(BF16)

    def spread(rows_ref, mid, back, ahead, r, z):
        value = rows_ref[r, z]
        if isinstance(r, int):
            ok = sx > 0 if r == 0 else sx < n_sx - 1
            value = jnp.where(ok, value.astype(F32), 0.0).astype(BF16)
        mid[r, z] = value.astype(F32)
        lhs = jnp.concatenate([value, halo[...]], axis=1)
        rhs = jnp.concatenate([turn[...], rim_matrix(rim_place(r, z))], axis=0)
        both = dot(lhs, rhs)
        back[r, z] = both[:, :NC]
        ahead[r, z] = both[:, NC:]

    def spread_all(which, rows_ref, mid, back, ahead, sent, recv):
        if comm:
            for slot in range(6):
                pack_copy(which, sent, recv, slot).wait_recv()
            halo[...] = rim(recv)
        else:
            halo[...] = jnp.zeros_like(halo)

        @pl.loop(1, NR + 1, unroll=4)
        def _(r):
            for z in range(2):
                spread(rows_ref, mid, back, ahead, r, z)

        if comm:
            slab_copy(which, rows_ref, 0).wait_recv()
            slab_copy(which, rows_ref, 1).wait_recv()
        else:
            rows_ref[0] = jnp.zeros_like(rows_ref[0])
            rows_ref[NR + 1] = jnp.zeros_like(rows_ref[0])
        for r in (0, NR + 1):
            for z in range(2):
                spread(rows_ref, mid, back, ahead, r, z)

    with jax.named_scope("rows of x"):
        swap[...] = swap_matrix()
        for k in range(3):
            loads[k].wait()

            @pl.loop(4 * k, 4 * k + 4, unroll=4)
            def _(b):
                part = xv[block_of(b, WIDE)]
                rhs = jnp.concatenate([part[:, z].reshape(WIDE * NR, NC) for z in range(2)], axis=1)
                both = dot(swap[...], rhs).astype(BF16)
                for i in range(NR):
                    for z in range(2):
                        xb[i + 1, z, block_of(b, WIDE), :] = both[WIDE * i : WIDE * (i + 1), NC * z : NC * (z + 1)]

    with jax.named_scope("send x"):
        pick = pick_matrix()
        for i in range(NR // 2):
            four = jnp.concatenate([xb[2 * i + 1 + k // 2, k % 2] for k in range(4)], axis=1)
            edge[i] = dot_nt(pick, four)
        pack_edges(px)
        if comm:
            pl.semaphore_wait(barrier, n_group - 1 + n_sx - 1 + 4)
            slab_copy(0, xb, 0).start()
            slab_copy(0, xb, 1).start()
        send_edges(0, px, prx)

    with jax.named_scope("constants"):
        for k in range(3, 7):
            loads[k].wait()
        turn[...] = shift_matrix()
        eye = one_hot(iota((CH, CH), 0) == iota((CH, CH), 1))
        mit[...] = dot_nt(eye, mi[...]).astype(BF16)
        mot[...] = dot_nt(eye, mo[...]).astype(BF16)

    with jax.named_scope("weights"):
        value = jnp.concatenate([dk[...], bias[...], jnp.zeros((100, CH), F32)], axis=0)
        value = jnp.concatenate([value, jnp.zeros((128, 64), F32)], axis=1).T[:CH]
        high = value.astype(BF16).astype(F32)
        middle = (value - high).astype(BF16).astype(F32)
        low = value - high - middle
        tall[...] = (high + pltpu.roll(middle, 32, axis=1) + pltpu.roll(low, 64, axis=1)).astype(BF16)

        @pl.loop(0, 14, unroll=2)
        def _(d):
            both = dot(tall[...], tap_matrix(d))
            w[2 * d] = both[:, :128]
            w[2 * d + 1] = both[:, 128:]

    loads[7].wait()
    with jax.named_scope("cotangent"):
        @pl.loop(0, CH // WIDE, unroll=4)
        def _(b):
            part = cv[block_of(b, WIDE)]
            rhs = jnp.concatenate([part[:, z].reshape(WIDE * NR, NC) for z in range(2)], axis=1)
            both = dot(swap[...], rhs).astype(BF16)
            for i in range(NR):
                cb[i // 2, block_of(b, WIDE), 256 * (i % 2) : 256 * (i % 2) + 256] = both[WIDE * i : WIDE * (i + 1)]

        @pl.loop(0, NR // 2, unroll=4)
        def _(i):
            ag[i] = dot(mot[...], cb[i])

    with jax.named_scope("spread x"):
        spread_all(0, xb, a0, am, ap, px, prx)

    with jax.named_scope("hidden"):
        @pl.loop(0, CH // BLK)
        def _(b):
            rows = block_of(b, BLK)

            def emit(i, first, second):
                at = 256 * (i % 2)
                hid[i // 2, rows, at : at + 128] = first
                hid[i // 2, rows, at + 128 : at + 256] = second

            stencil_block(a0, am, ap, w, False, rows, emit)

    with jax.named_scope("chain"):
        moa[...] = jnp.zeros_like(moa)
        mia[...] = jnp.zeros_like(mia)

        @pl.loop(0, NR // 2, unroll=4)
        def _(i):
            hidden = hid[i].astype(BF16)
            shift = w[27]
            pre = dot(mi[...], hidden) + jnp.concatenate([shift] * 4, axis=1)
            cdf = 0.5 * (1.0 + lax.erf(pre * INV_SQRT2))
            dens = jnp.exp(-0.5 * pre * pre) * INV_SQRT2PI
            act = (pre * cdf).astype(BF16)
            pg = (ag[i] * (cdf + pre * dens)).astype(BF16)
            moa[...] += dot_nt(cb[i], act)
            mia[...] += dot_nt(pg, jnp.concatenate([hidden, jnp.ones((16, 4 * NC), BF16)], axis=0))
            hg = dot(mit[...], pg).astype(BF16)
            for k in range(4):
                piece = hg[:, NC * k : NC * (k + 1)]
                hb[2 * i + 1 + k // 2, k % 2] = piece
                b0[2 * i + 1 + k // 2, k % 2] = piece.astype(F32)
            edge[i] = dot_nt(pick_matrix(), hg)

    with jax.named_scope("send grad"):
        if comm:
            slab_copy(1, hb, 0).start()
            slab_copy(1, hb, 1).start()
        pack_edges(ph)
        send_edges(1, ph, prh)

    def scatter(g):
        return pltpu.make_async_remote_copy(
            src_ref=gs.at[g], dst_ref=ar.at[me], send_sem=asend.at[g], recv_sem=arecv.at[me],
            device_id=at_group(g), device_id_type=MESH,
        )

    def share(d):
        return pltpu.make_async_remote_copy(
            src_ref=bs, dst_ref=br.at[sx], send_sem=bsend.at[d], recv_sem=brecv.at[sx],
            device_id=around(d, 0), device_id_type=MESH,
        )

    def publish(g):
        return pltpu.make_async_remote_copy(
            src_ref=fin.at[me], dst_ref=fin.at[me], send_sem=csend.at[g], recv_sem=crecv.at[me],
            device_id=at_group(g), device_id_type=MESH,
        )

    def arrived(ref, sem, slot):
        pltpu.make_async_remote_copy(
            src_ref=ref.at[slot], dst_ref=ref.at[slot], send_sem=asend.at[0], recv_sem=sem.at[slot],
            device_id=around(1, 0), device_id_type=MESH,
        ).wait_recv()

    def scatter_all(first, last):
        if comm:
            for d in range(1, n_group):
                g = lax.rem(me + d, n_group)

                @pl.when((g >= first) & (g < last))
                def _():
                    scatter(g).start()

    def sum_group(first, last):
        if comm:
            @pl.when((me >= first) & (me < last))
            def _():
                for d in range(1, n_group):
                    arrived(ar, arecv, lax.rem(me + d, n_group))
                ar[me] = gs[me]
                total = ar[0].astype(F32)
                for g in range(1, n_group):
                    total = total + ar[g].astype(F32)
                bs[...] = total.astype(BF16)
                for d in range(1, n_sx):
                    share(d).start()
                br[sx] = total.astype(BF16)

    def sum_rest(first, last):
        if comm:
            @pl.when((me >= first) & (me < last))
            def _():
                for d in range(1, n_sx):
                    arrived(br, brecv, lax.rem(sx + d, n_sx))
                total = br[0].astype(F32)
                for k in range(1, n_sx):
                    total = total + br[k].astype(F32)
                fin[me] = total.astype(BF16)
                for d in range(1, n_group):
                    publish(lax.rem(me + d, n_group)).start()

    with jax.named_scope("scatter mixes"):
        for rg in range(4):
            at = pl.ds(rg * CHUNK, CHUNK)
            gs[rg] = moa[at, 0:128].astype(BF16)
            gs[4 + rg] = jnp.concatenate([moa[at, 128:192], mia[at, 0:64]], axis=1).astype(BF16)
            gs[8 + rg] = mia[at, 64:192].astype(BF16)
        scatter_all(0, MIXES)

    with jax.named_scope("tap sums"):
        @pl.loop(0, CH // BLK)
        def _(b):
            rows = block_of(b, BLK)
            for k, value in enumerate(tap_sums_block(b0, a0, am, ap, rows)):
                acc[k, rows, :] = value

        acc[27] = jnp.where(iota((CH, NC), 1) == 0, mia[:, 192:193], 0.0)

        @pl.loop(0, 28, unroll=4)
        def _(k):
            value = acc[k]
            high = value.astype(BF16)
            low = (value - high.astype(F32)).astype(BF16)
            flat[k] = dot_nt(jnp.ones((8, 2 * NC), BF16), jnp.concatenate([high, low], axis=1))

    with jax.named_scope("scatter taps"):
        value = jnp.concatenate([flat[k, 0:1] for k in range(28)] + [jnp.zeros((20, CH), F32)], axis=0)
        gs[12] = value[:, 0:128].astype(BF16)
        gs[13] = jnp.concatenate([value[:, 128:192], jnp.zeros((CHUNK, 64), F32)], axis=1).astype(BF16)
        scatter_all(MIXES, CHUNKS)

    with jax.named_scope("spread grad"):
        spread_all(1, hb, b0, bm, bp, ph, prh)

    with jax.named_scope("sum mixes"):
        sum_group(0, MIXES)

    def input_grad(part):
        @pl.loop(8 * part, 8 * part + 8)
        def _(b):
            rows = block_of(b, BLK)

            def emit(i, first, second):
                at = 256 * (i % 2)
                ag[i // 2, rows, at : at + 128] = first
                ag[i // 2, rows, at + 128 : at + 256] = second

            stencil_block(b0, bm, bp, w, True, rows, emit)

        @pl.loop(4 * part, 4 * part + 4, unroll=4)
        def _(b):
            rows = block_of(b, WIDE)
            rhs = [ag[i // 2, rows, 256 * (i % 2) : 256 * (i % 2) + 256].astype(BF16) for i in range(NR)]
            both = dot(swap[...], jnp.concatenate(rhs, axis=0))
            for z in range(2):
                value = both[:, NC * z : NC * (z + 1)].reshape(WIDE, NR, NC)
                ov[rows, z] = (cv[rows, z].astype(F32) + value).astype(BF16)

    def save_part(part):
        at = pl.ds(third * part, third)
        return pltpu.make_async_copy(ov.at[at], ig_hbm.at[at], save.at[part])

    with jax.named_scope("grad 1"):
        input_grad(0)
    save_part(0).start()
    with jax.named_scope("sum taps"):
        sum_group(MIXES, CHUNKS)
        sum_rest(0, MIXES)
    with jax.named_scope("grad 2"):
        input_grad(1)
    save_part(1).start()
    with jax.named_scope("sum taps 2"):
        sum_rest(MIXES, CHUNKS)
    with jax.named_scope("grad 3"):
        input_grad(2)
    save_part(2).start()

    with jax.named_scope("finish"):
        if comm:
            for which, rows_ref, sent, recv in ((0, xb, px, prx), (1, hb, ph, prh)):
                for slot in range(6):
                    pack_copy(which, sent, recv, slot).wait_send()
                slab_copy(which, rows_ref, 0).wait_send()
                slab_copy(which, rows_ref, 1).wait_send()
            for g in range(CHUNKS):
                @pl.when(me != g)
                def _():
                    scatter(g).wait_send()
                    arrived(fin, crecv, g)

            @pl.when(me < CHUNKS)
            def _():
                for d in range(1, n_sx):
                    share(d).wait_send()
                for d in range(1, n_group):
                    publish(lax.rem(me + d, n_group)).wait_send()
        else:
            fin[...] = gs[...]
        sums_ref[...] = fin[...].astype(F32) * factor
        for part in range(3):
            save_part(part).wait()


def deliver(ig_in, sums_ref, ig_out, kg_ref, mig_ref, bg_ref, mog_ref, held, sems):
    parts = ig_in.shape[0] // 4
    at = [pl.ds(parts * k, parts) for k in range(4)]
    inward = [pltpu.make_async_copy(ig_in.at[at[k]], held.at[at[k]], sems.at[0, k]) for k in range(4)]
    outward = [pltpu.make_async_copy(held.at[at[k]], ig_out.at[at[k]], sems.at[1, k]) for k in range(4)]
    for copy in inward:
        copy.start()
    for rg in range(4):
        rows = pl.ds(rg * CHUNK, CHUNK)
        mog_ref[rows, 0:128] = sums_ref[rg]
        mog_ref[rows, 128:192] = sums_ref[4 + rg, :, 0:64]
        mig_ref[rows, 0:64] = sums_ref[4 + rg, :, 64:128]
        mig_ref[rows, 64:192] = sums_ref[8 + rg]
    kg_ref[:, 0:128] = sums_ref[12, 0:27]
    kg_ref[:, 128:192] = sums_ref[13, 0:27, 0:64]
    bg_ref[:, 0:128] = sums_ref[12, 27:28]
    bg_ref[:, 128:192] = sums_ref[13, 27:28, 0:64]
    for first, second in zip(inward, outward):
        first.wait()
        second.start()
    for copy in outward:
        copy.wait()


def per_device(sizes, factor, inputs, cotangent, depth_kernel, mix_in, mix_bias, mix_out):
    tile = (CH, 2, NR, NC)
    vm = pltpu.VMEM
    field = (RR, 2, CH, NC)
    pairs = (NR // 2, CH, 4 * NC)
    dma = pltpu.SemaphoreType.DMA
    n_sx, n_sy, n_sample = sizes
    sums = (CHUNKS, CHUNK, 128)
    scratch = [
        vm(tile, BF16), vm(tile, BF16), vm(tile, BF16),
        vm((27, CH), F32), vm((1, CH), F32), vm((CH, CH), BF16), vm((CH, CH), BF16),
        vm(field, BF16), vm(field, BF16),
        vm(field, F32), vm(field, F32), vm(field, F32),
        vm(field, F32), vm(field, F32), vm(field, F32),
        vm(pairs, BF16), vm(pairs, F32), vm(pairs, F32),
        vm((28, CH, 128), F32), vm((28, CH, 128), F32),
        vm((CH, CH), BF16), vm((CH, CH), BF16), vm((NC, 2 * NC), BF16), vm((256, 256), BF16),
        vm((4, 16, CH), BF16), vm((4, 16, CH), BF16), vm((6, 4, 16, CH), BF16), vm((6, 4, 16, CH), BF16),
        vm((NR // 2, 8, CH), F32), vm((CH, 128), BF16),
        vm((CH, CH), F32), vm((CH, CH + 16), F32), vm((CH, 128), BF16), vm((28, 8, CH), F32),
        vm(sums, BF16), vm((16, CHUNK, 128), BF16), vm((8, CHUNK, 128), BF16),
        vm(sums, BF16), vm((CHUNK, 128), BF16),
        dma((8,)), dma((3,)), dma((2, 8)), dma((2, 8)),
        dma((16,)), dma((16,)), dma((8,)), dma((8,)), dma((16,)), dma((16,)),
    ]
    here = pl.BlockSpec(memory_space=pltpu.VMEM)
    there = pl.BlockSpec(memory_space=pl.ANY)
    params = dict(vmem_limit_bytes=60 * 1024 * 1024)
    if n_sx > 1:
        params.update(collective_id=0, has_side_effects=True)
    ig, sums = pl.pallas_call(
        functools.partial(kernel, sizes, factor),
        out_shape=(jax.ShapeDtypeStruct(tile, BF16), jax.ShapeDtypeStruct(sums, F32)),
        in_specs=[there] * 6,
        out_specs=(there, here),
        scratch_shapes=scratch,
        compiler_params=pltpu.CompilerParams(**params),
        name="block",
    )(
        inputs.reshape(tile),
        cotangent.reshape(tile),
        depth_kernel.T,
        mix_bias.reshape(1, CH),
        mix_in,
        mix_out,
    )
    ig, kg, mig, bg, mog = pl.pallas_call(
        deliver,
        out_shape=(
            jax.ShapeDtypeStruct(tile, BF16),
            jax.ShapeDtypeStruct((27, CH), F32),
            jax.ShapeDtypeStruct((CH, CH), F32),
            jax.ShapeDtypeStruct((1, CH), F32),
            jax.ShapeDtypeStruct((CH, CH), F32),
        ),
        in_specs=[there, here],
        out_specs=(there, here, here, here, here),
        scratch_shapes=[vm(tile, BF16), dma((2, 4))],
        name="deliver",
    )(ig, sums)
    return (ig.reshape(inputs.shape), kg.T, mig, bg.reshape(CH), mog)


def solution(mesh):
    sizes = tuple(mesh.shape[a] for a in ("sx", "sy", "sample"))
    cells = sizes[0] * sizes[1] * sizes[2] * 2 * NR * NC
    field = P("sample", None, None, "sx", "sy")
    return jax.shard_map(
        functools.partial(per_device, sizes, 1.0 / math.sqrt(cells)),
        mesh=mesh,
        in_specs=(field, field, P(), P(), P(), P()),
        out_specs=(field, P(), P(), P(), P()),
        check_vma=False,
    )
```

time: 358 us -> 48 us (0.13)
  waiting for transfers between devices: 113 us -> 0 us
  blocking collectives: 68.7 us -> 0 us
  other arithmetic: 61.6 us -> 0 us
  Pallas kernels: 0 us -> 47.1 us
  matrix products: 38.9 us -> 0 us
  local copies, waits for them, and re-layouts: 36.1 us -> 0 us
  starting transfers between devices: 22.9 us -> 0 us
  between operations: 15.1 us -> 0.64 us
    psum x1 -> x0, waiting for transfers between devices: 111 us -> none  [per_device(): lax.psum((kern_sum, in_sum, bias_sum, out_sum), ('sx', 'sy', 'sample'))]
    psum x1 -> x0, blocking collectives: 68.7 us -> none  [per_device(): lax.psum((kern_sum, in_sum, bias_sum, out_sum), ('sx', 'sy', 'sample'))]
    pallas_call x0 -> x2, Pallas kernels: none -> 47.1 us  [the longest x1 43.2 us: per_device(): pl.pallas_call(functools.partial(kernel, sizes, factor), out_shape=(jax.S...]
    dot_general x5 -> x0, matrix products: 38.9 us -> none  [the longest x1 29.3 us: chain(): jnp.einsum('oc,bozxy->bczxy', mix_in, pre_grad, preferred_element_type=jn...]
    ppermute x8 -> x0, starting transfers between devices: 22.9 us -> none  [the longest x4 16.5 us: extended(): lax.ppermute(tail, axis, [(i, (i + 1) % count) for i in range(ends)])]
    another operation x1 -> x0, other arithmetic: 17 us -> none
    slice x10 -> x0, local copies, waits for them, and re-layouts: 16.7 us -> none  [the longest x6 10.3 us: extended(): lax.slice_in_dim(cells, cells.shape[dim] - width, cells.shape[dim], axis=...]
    convert_element_type x1 -> x0, other arithmetic: 15.2 us -> none  [per_device(): input_grad = (cotangent.astype(jnp.float32) + spread).astype(jnp.bfloat16)]
  transfers between devices with their start and end apart: 9 -> 0, of which waited for: 2 -> 0; matrix products, arithmetic and copies ran while one was open for 15% -> 0% of each run, Pallas kernels for 0% -> 0%
where the time goes in v2:
time: 48 us; the launch traced here: 47.8 us
  Pallas kernels  47.1 us (98%)
  between operations  0.64 us (1%)
    pallas_call x1, Pallas kernels, per_device(): pl.pallas_call(functools.partial(kernel, sizes, factor), out_shape=(jax.S...  43.2 us
    pallas_call x1, Pallas kernels, per_device(): pl.pallas_call(deliver, out_shape=(jax.ShapeDtypeStruct(tile, BF16), jax....  3.94 us

profile of v2, /device:TPU:1, one launch (start us, length us, event | category | flops | bytes accessed | tf_op | source)
XLA Modules:
  0.0 47.8 jit_solution(2827809707165068859)
XLA Ops:
  0.6 43.2 %block.1 = (bf16[192,2,16,128]{3,2,1,0:T(8,128)(2,1)}, f32[14,48,128]{2,1,0:T(8,128)}) custom-call(bf16[192,2,16,128]{3,2,1,0:T(8,128)(2,1)} %bitcast.7, bf16[192,2,16,128]{3,2,1,0:T(8,128)(2,1)} %bitcast.8, f32[27,192]{1,0:T(8,128)} %bitcast.9, f32[1,192]{1,0:T(1,128)} %bitcast.10, bf16[192,192]{1,0:T(8,128)(2,1)} %mi_hbm.1, bf16[192,192]{1,0:T(8,128)(2,1)} %mo_hbm.1), custom_call_target="tpu_custom_call" | custom-call | tf_op jit(solution)/shard_map/block/pallas_call | solution.py:581
  43.8 3.9 %deliver.1 = (bf16[192,2,16,128]{3,2,1,0:T(8,128)(2,1)}, f32[27,192]{1,0:T(8,128)}, f32[192,192]{1,0:T(8,128)}, f32[1,192]{1,0:T(1,128)}, f32[192,192]{1,0:T(8,128)}) custom-call(bf16[192,2,16,128]{3,2,1,0:T(8,128)(2,1)} %get-tuple-element.12.ig_in, f32[14,48,128]{2,1,0:T(8,128)} %get-tuple-element.13.sums_ref), custom_call_target="tpu_custom_call" | custom-call | tf_op jit(solution)/shard_map/deliver/pallas_call | solution.py:597

commit v3 on v2

--- a/solution.py
+++ b/solution.py
@@ -21,8 +21,8 @@
 BLK = 8
 WIDE = 16
 CHUNK = 48
-MIXES = 12
-CHUNKS = 14
+PIECE = 80
+PARTS = 8
 
 
 def dot(a, b):
@@ -134,11 +134,11 @@
 def kernel(
     sizes, factor,
     x_hbm, cot_hbm, dk_hbm, bias_hbm, mi_hbm, mo_hbm,
-    ig_hbm, sums_ref,
-    xv, cv, ov, dk, bias, mi, mo,
+    ig_hbm, sums_hbm,
+    xv, cv, ov, sums_ref, dk, bias, mi, mo,
     xb, hb, a0, am, ap, b0, bm, bp, cb, ag, hid, w, acc, mit, mot, turn, swap,
-    px, ph, prx, prh, edge, halo, moa, mia, tall, flat, gs, ar, br, fin, bs,
-    load, save, hsend, hrecv, asend, arecv, bsend, brecv, csend, crecv,
+    px, ph, prx, prh, edge, halo, moa, mia, tall, flat, gs, ar, br, fin, bs, pgs, ks, kr, kt, kg,
+    load, save, hsend, hrecv, asend, arecv, bsend, brecv, csend, crecv, ksend, krecv, lsend, lrecv,
 ):
     n_sx, n_sy, n_sample = sizes
     comm = n_sx > 1
@@ -163,7 +163,7 @@
         for k, (src, dst) in enumerate(((mi_hbm, mi), (mo_hbm, mo), (dk_hbm, dk), (bias_hbm, bias), (cot_hbm, cv)))
     ]
     with jax.named_scope("start"):
-        for copy in loads:
+        for copy in loads[:7]:
             copy.start()
         if comm:
             barrier = pltpu.get_barrier_semaphore()
@@ -188,10 +188,11 @@
             device_id=around(dx, dy), device_id_type=MESH,
         )
 
-    def slab_copy(which, ref, up):
+    def slab_copy(which, ref, up, k):
+        part = pl.ds(third * k, third)
         return pltpu.make_async_remote_copy(
-            src_ref=ref.at[NR if up else 1], dst_ref=ref.at[0 if up else NR + 1],
-            send_sem=hsend.at[which, 6 + up], recv_sem=hrecv.at[which, 6 + up],
+            src_ref=ref.at[NR if up else 1, :, part], dst_ref=ref.at[0 if up else NR + 1, :, part],
+            send_sem=hsend.at[which, 6 + 3 * up + k], recv_sem=hrecv.at[which, 6 + 3 * up + k],
             device_id=around(1 if up else -1, 0), device_id_type=MESH,
         )
 
@@ -246,8 +247,9 @@
                 spread(rows_ref, mid, back, ahead, r, z)
 
         if comm:
-            slab_copy(which, rows_ref, 0).wait_recv()
-            slab_copy(which, rows_ref, 1).wait_recv()
+            for k in range(3):
+                slab_copy(which, rows_ref, 0, k).wait_recv()
+                slab_copy(which, rows_ref, 1, k).wait_recv()
         else:
             rows_ref[0] = jnp.zeros_like(rows_ref[0])
             rows_ref[NR + 1] = jnp.zeros_like(rows_ref[0])
@@ -269,16 +271,19 @@
                     for z in range(2):
                         xb[i + 1, z, block_of(b, WIDE), :] = both[WIDE * i : WIDE * (i + 1), NC * z : NC * (z + 1)]
 
+            if comm:
+                if k == 0:
+                    pl.semaphore_wait(barrier, n_group - 1 + n_sx - 1 + 4)
+                slab_copy(0, xb, 0, k).start()
+                slab_copy(0, xb, 1, k).start()
+        loads[7].start()
+
     with jax.named_scope("send x"):
         pick = pick_matrix()
         for i in range(NR // 2):
             four = jnp.concatenate([xb[2 * i + 1 + k // 2, k % 2] for k in range(4)], axis=1)
             edge[i] = dot_nt(pick, four)
         pack_edges(px)
-        if comm:
-            pl.semaphore_wait(barrier, n_group - 1 + n_sx - 1 + 4)
-            slab_copy(0, xb, 0).start()
-            slab_copy(0, xb, 1).start()
         send_edges(0, px, prx)
 
     with jax.named_scope("constants"):
@@ -297,7 +302,7 @@
         low = value - high - middle
         tall[...] = (high + pltpu.roll(middle, 32, axis=1) + pltpu.roll(low, 64, axis=1)).astype(BF16)
 
-        @pl.loop(0, 14, unroll=2)
+        @pl.loop(0, 14, unroll=7)
         def _(d):
             both = dot(tall[...], tap_matrix(d))
             w[2 * d] = both[:, :128]
@@ -347,7 +352,85 @@
             pg = (ag[i] * (cdf + pre * dens)).astype(BF16)
             moa[...] += dot_nt(cb[i], act)
             mia[...] += dot_nt(pg, jnp.concatenate([hidden, jnp.ones((16, 4 * NC), BF16)], axis=0))
-            hg = dot(mit[...], pg).astype(BF16)
+            pgs[i] = pg
+
+    def over_sx(src, dst, sends, recvs, d):
+        return pltpu.make_async_remote_copy(
+            src_ref=src, dst_ref=dst.at[sx], send_sem=sends.at[d], recv_sem=recvs.at[sx],
+            device_id=around(d, 0), device_id_type=MESH,
+        )
+
+    def over_group(src, dst, sends, recvs, d):
+        return pltpu.make_async_remote_copy(
+            src_ref=src, dst_ref=dst.at[me], send_sem=sends.at[d], recv_sem=recvs.at[me],
+            device_id=at_group(lax.rem(me + d, n_group)), device_id_type=MESH,
+        )
+
+    def scatter(d):
+        return over_sx(gs.at[lax.rem(sx + d, n_sx)], ar, asend, arecv, d)
+
+    def publish(d):
+        return over_sx(fin.at[sx], fin, csend, crecv, d)
+
+    def arrived(ref, sem, slot):
+        pltpu.make_async_remote_copy(
+            src_ref=ref.at[slot], dst_ref=ref.at[slot], send_sem=asend.at[0], recv_sem=sem.at[slot],
+            device_id=around(1, 0), device_id_type=MESH,
+        ).wait_recv()
+
+    def arrived_sx(ref, sem):
+        for d in range(1, n_sx):
+            arrived(ref, sem, lax.rem(sx + d, n_sx))
+
+    def arrived_group(ref, sem):
+        for d in range(1, n_group):
+            arrived(ref, sem, lax.rem(me + d, n_group))
+
+    def added(ref, count):
+        total = ref[0].astype(F32)
+        for k in range(1, count):
+            total = total + ref[k].astype(F32)
+        return total
+
+    def sum_sx():
+        if comm:
+            arrived_sx(ar, arecv)
+            ar[sx] = gs[sx]
+            bs[...] = added(ar, n_sx).astype(BF16)
+            for d in range(1, n_group):
+                over_group(bs, br, bsend, brecv, d).start()
+            br[me] = bs[...]
+
+    def sum_group():
+        if comm:
+            arrived_group(br, brecv)
+            fin[sx] = added(br, n_group).astype(BF16)
+            for d in range(1, n_sx):
+                publish(d).start()
+
+    def sum_taps():
+        if comm:
+            arrived_sx(kr, krecv)
+            kr[sx] = ks[...]
+            kt[...] = added(kr, n_sx).astype(BF16)
+            for d in range(1, n_group):
+                over_group(kt, kg, lsend, lrecv, d).start()
+            kg[me] = kt[...]
+
+    with jax.named_scope("scatter mixes"):
+        for k in range(PARTS):
+            at = pl.ds(24 * k, 24)
+            mid = jnp.concatenate([moa[at, 128:192], mia[at, 0:64]], axis=1)
+            value = jnp.concatenate([moa[at, 0:128], mid, mia[at, 64:192], jnp.zeros((8, 128), F32)], axis=0)
+            gs[k] = value.astype(BF16)
+        if comm:
+            for d in range(1, n_sx):
+                scatter(d).start()
+
+    with jax.named_scope("hidden grad"):
+        @pl.loop(0, NR // 2, unroll=4)
+        def _(i):
+            hg = dot(mit[...], pgs[i]).astype(BF16)
             for k in range(4):
                 piece = hg[:, NC * k : NC * (k + 1)]
                 hb[2 * i + 1 + k // 2, k % 2] = piece
@@ -356,107 +439,43 @@
 
     with jax.named_scope("send grad"):
         if comm:
-            slab_copy(1, hb, 0).start()
-            slab_copy(1, hb, 1).start()
+            for k in range(3):
+                slab_copy(1, hb, 0, k).start()
+                slab_copy(1, hb, 1, k).start()
         pack_edges(ph)
         send_edges(1, ph, prh)
 
-    def scatter(g):
-        return pltpu.make_async_remote_copy(
-            src_ref=gs.at[g], dst_ref=ar.at[me], send_sem=asend.at[g], recv_sem=arecv.at[me],
-            device_id=at_group(g), device_id_type=MESH,
-        )
-
-    def share(d):
-        return pltpu.make_async_remote_copy(
-            src_ref=bs, dst_ref=br.at[sx], send_sem=bsend.at[d], recv_sem=brecv.at[sx],
-            device_id=around(d, 0), device_id_type=MESH,
-        )
-
-    def publish(g):
-        return pltpu.make_async_remote_copy(
-            src_ref=fin.at[me], dst_ref=fin.at[me], send_sem=csend.at[g], recv_sem=crecv.at[me],
-            device_id=at_group(g), device_id_type=MESH,
-        )
-
-    def arrived(ref, sem, slot):
-        pltpu.make_async_remote_copy(
-            src_ref=ref.at[slot], dst_ref=ref.at[slot], send_sem=asend.at[0], recv_sem=sem.at[slot],
-            device_id=around(1, 0), device_id_type=MESH,
-        ).wait_recv()
-
-    def scatter_all(first, last):
-        if comm:
-            for d in range(1, n_group):
-                g = lax.rem(me + d, n_group)
-
-                @pl.when((g >= first) & (g < last))
-                def _():
-                    scatter(g).start()
-
-    def sum_group(first, last):
-        if comm:
-            @pl.when((me >= first) & (me < last))
-            def _():
-                for d in range(1, n_group):
-                    arrived(ar, arecv, lax.rem(me + d, n_group))
-                ar[me] = gs[me]
-                total = ar[0].astype(F32)
-                for g in range(1, n_group):
-                    total = total + ar[g].astype(F32)
-                bs[...] = total.astype(BF16)
-                for d in range(1, n_sx):
-                    share(d).start()
-                br[sx] = total.astype(BF16)
-
-    def sum_rest(first, last):
-        if comm:
-            @pl.when((me >= first) & (me < last))
-            def _():
-                for d in range(1, n_sx):
-                    arrived(br, brecv, lax.rem(sx + d, n_sx))
-                total = br[0].astype(F32)
-                for k in range(1, n_sx):
-                    total = total + br[k].astype(F32)
-                fin[me] = total.astype(BF16)
-                for d in range(1, n_group):
-                    publish(lax.rem(me + d, n_group)).start()
-
-    with jax.named_scope("scatter mixes"):
-        for rg in range(4):
-            at = pl.ds(rg * CHUNK, CHUNK)
-            gs[rg] = moa[at, 0:128].astype(BF16)
-            gs[4 + rg] = jnp.concatenate([moa[at, 128:192], mia[at, 0:64]], axis=1).astype(BF16)
-            gs[8 + rg] = mia[at, 64:192].astype(BF16)
-        scatter_all(0, MIXES)
-
-    with jax.named_scope("tap sums"):
-        @pl.loop(0, CH // BLK)
+    def tap_sums(start, stop):
+        @pl.loop(start, stop)
         def _(b):
             rows = block_of(b, BLK)
             for k, value in enumerate(tap_sums_block(b0, a0, am, ap, rows)):
                 acc[k, rows, :] = value
 
+    with jax.named_scope("tap sums"):
+        tap_sums(0, 14)
+    with jax.named_scope("sum sx"):
+        sum_sx()
+    with jax.named_scope("tap sums 2"):
+        tap_sums(14, 24)
         acc[27] = jnp.where(iota((CH, NC), 1) == 0, mia[:, 192:193], 0.0)
 
-        @pl.loop(0, 28, unroll=4)
-        def _(k):
+        for k in range(28):
             value = acc[k]
             high = value.astype(BF16)
             low = (value - high.astype(F32)).astype(BF16)
             flat[k] = dot_nt(jnp.ones((8, 2 * NC), BF16), jnp.concatenate([high, low], axis=1))
 
     with jax.named_scope("scatter taps"):
-        value = jnp.concatenate([flat[k, 0:1] for k in range(28)] + [jnp.zeros((20, CH), F32)], axis=0)
-        gs[12] = value[:, 0:128].astype(BF16)
-        gs[13] = jnp.concatenate([value[:, 128:192], jnp.zeros((CHUNK, 64), F32)], axis=1).astype(BF16)
-        scatter_all(MIXES, CHUNKS)
+        value = jnp.concatenate([flat[k, 0:1] for k in range(28)] + [jnp.zeros((4, CH), F32)], axis=0)
+        ks[0:32] = value[:, 0:128].astype(BF16)
+        ks[32:48] = jnp.concatenate([value[0:16, 128:192], value[16:32, 128:192]], axis=1).astype(BF16)
+        if comm:
+            for d in range(1, n_sx):
+                over_sx(ks, kr, ksend, krecv, d).start()
 
     with jax.named_scope("spread grad"):
         spread_all(1, hb, b0, bm, bp, ph, prh)
-
-    with jax.named_scope("sum mixes"):
-        sum_group(0, MIXES)
 
     def input_grad(part):
         @pl.loop(8 * part, 8 * part + 8)
@@ -486,14 +505,12 @@
     with jax.named_scope("grad 1"):
         input_grad(0)
     save_part(0).start()
-    with jax.named_scope("sum taps"):
-        sum_group(MIXES, CHUNKS)
-        sum_rest(0, MIXES)
+    with jax.named_scope("sum rest"):
+        sum_taps()
+        sum_group()
     with jax.named_scope("grad 2"):
         input_grad(1)
     save_part(1).start()
-    with jax.named_scope("sum taps 2"):
-        sum_rest(MIXES, CHUNKS)
     with jax.named_scope("grad 3"):
         input_grad(2)
     save_part(2).start()
@@ -503,48 +520,60 @@
             for which, rows_ref, sent, recv in ((0, xb, px, prx), (1, hb, ph, prh)):
                 for slot in range(6):
                     pack_copy(which, sent, recv, slot).wait_send()
-                slab_copy(which, rows_ref, 0).wait_send()
-                slab_copy(which, rows_ref, 1).wait_send()
-            for g in range(CHUNKS):
-                @pl.when(me != g)
-                def _():
-                    scatter(g).wait_send()
-                    arrived(fin, crecv, g)
-
-            @pl.when(me < CHUNKS)
-            def _():
-                for d in range(1, n_sx):
-                    share(d).wait_send()
-                for d in range(1, n_group):
-                    publish(lax.rem(me + d, n_group)).wait_send()
+                for k in range(3):
+                    slab_copy(which, rows_ref, 0, k).wait_send()
+                    slab_copy(which, rows_ref, 1, k).wait_send()
+            for d in range(1, n_sx):
+                scatter(d).wait_send()
+                over_sx(ks, kr, ksend, krecv, d).wait_send()
+                publish(d).wait_send()
+            for d in range(1, n_group):
+                over_group(bs, br, bsend, brecv, d).wait_send()
+                over_group(kt, kg, lsend, lrecv, d).wait_send()
+            arrived_sx(fin, crecv)
+            arrived_group(kg, lrecv)
+            sums_ref[PARTS, 0:CHUNK] = added(kg, n_group) * factor
         else:
             fin[...] = gs[...]
-        sums_ref[...] = fin[...].astype(F32) * factor
+            sums_ref[PARTS, 0:CHUNK] = ks[...].astype(F32) * factor
+        sums_ref[PARTS, CHUNK:PIECE] = jnp.zeros((PIECE - CHUNK, 128), F32)
+        sums_ref[0:PARTS] = fin[...].astype(F32) * factor
+        last = pltpu.make_async_copy(sums_ref, sums_hbm, save.at[3])
+        last.start()
         for part in range(3):
             save_part(part).wait()
-
-
-def deliver(ig_in, sums_ref, ig_out, kg_ref, mig_ref, bg_ref, mog_ref, held, sems):
-    parts = ig_in.shape[0] // 4
+        last.wait()
+
+
+def deliver(ig_in, sums_in, ig_out, kg_out, mig_out, bg_out, mog_out, held, sums, kg, mig, bg, mog, sems):
+    parts = CH // 4
     at = [pl.ds(parts * k, parts) for k in range(4)]
     inward = [pltpu.make_async_copy(ig_in.at[at[k]], held.at[at[k]], sems.at[0, k]) for k in range(4)]
     outward = [pltpu.make_async_copy(held.at[at[k]], ig_out.at[at[k]], sems.at[1, k]) for k in range(4)]
+    first = pltpu.make_async_copy(sums_in, sums, sems.at[0, 4])
+    first.start()
     for copy in inward:
         copy.start()
-    for rg in range(4):
-        rows = pl.ds(rg * CHUNK, CHUNK)
-        mog_ref[rows, 0:128] = sums_ref[rg]
-        mog_ref[rows, 128:192] = sums_ref[4 + rg, :, 0:64]
-        mig_ref[rows, 0:64] = sums_ref[4 + rg, :, 64:128]
-        mig_ref[rows, 64:192] = sums_ref[8 + rg]
-    kg_ref[:, 0:128] = sums_ref[12, 0:27]
-    kg_ref[:, 128:192] = sums_ref[13, 0:27, 0:64]
-    bg_ref[:, 0:128] = sums_ref[12, 27:28]
-    bg_ref[:, 128:192] = sums_ref[13, 27:28, 0:64]
-    for first, second in zip(inward, outward):
-        first.wait()
-        second.start()
-    for copy in outward:
+    first.wait()
+    for k in range(PARTS):
+        rows = pl.ds(24 * k, 24)
+        mog[rows, 0:128] = sums[k, 0:24]
+        mog[rows, 128:192] = sums[k, 24:48, 0:64]
+        mig[rows, 0:64] = sums[k, 24:48, 64:128]
+        mig[rows, 64:192] = sums[k, 48:72]
+    kg[:, 0:128] = sums[PARTS, 0:27]
+    kg[0:16, 128:192] = sums[PARTS, 32:48, 0:64]
+    kg[16:27, 128:192] = sums[PARTS, 32:43, 64:128]
+    bg[:, 0:128] = sums[PARTS, 27:28]
+    bg[:, 128:192] = sums[PARTS, 43:44, 64:128]
+    pairs = ((kg, kg_out), (mig, mig_out), (bg, bg_out), (mog, mog_out))
+    small = [pltpu.make_async_copy(src, dst, sems.at[1, 4 + k]) for k, (src, dst) in enumerate(pairs)]
+    for copy in small:
+        copy.start()
+    for k in range(4):
+        inward[k].wait()
+        outward[k].start()
+    for copy in outward + small:
         copy.wait()
 
 
@@ -555,9 +584,9 @@
     pairs = (NR // 2, CH, 4 * NC)
     dma = pltpu.SemaphoreType.DMA
     n_sx, n_sy, n_sample = sizes
-    sums = (CHUNKS, CHUNK, 128)
+    sums = (PARTS + 1, PIECE, 128)
     scratch = [
-        vm(tile, BF16), vm(tile, BF16), vm(tile, BF16),
+        vm(tile, BF16), vm(tile, BF16), vm(tile, BF16), vm(sums, F32),
         vm((27, CH), F32), vm((1, CH), F32), vm((CH, CH), BF16), vm((CH, CH), BF16),
         vm(field, BF16), vm(field, BF16),
         vm(field, F32), vm(field, F32), vm(field, F32),
@@ -568,12 +597,13 @@
         vm((4, 16, CH), BF16), vm((4, 16, CH), BF16), vm((6, 4, 16, CH), BF16), vm((6, 4, 16, CH), BF16),
         vm((NR // 2, 8, CH), F32), vm((CH, 128), BF16),
         vm((CH, CH), F32), vm((CH, CH + 16), F32), vm((CH, 128), BF16), vm((28, 8, CH), F32),
-        vm(sums, BF16), vm((16, CHUNK, 128), BF16), vm((8, CHUNK, 128), BF16),
-        vm(sums, BF16), vm((CHUNK, 128), BF16),
-        dma((8,)), dma((3,)), dma((2, 8)), dma((2, 8)),
-        dma((16,)), dma((16,)), dma((8,)), dma((8,)), dma((16,)), dma((16,)),
+        vm((PARTS, PIECE, 128), BF16), vm((PARTS, PIECE, 128), BF16), vm((16, PIECE, 128), BF16),
+        vm((PARTS, PIECE, 128), BF16), vm((PIECE, 128), BF16), vm(pairs, BF16),
+        vm((CHUNK, 128), BF16), vm((8, CHUNK, 128), BF16), vm((CHUNK, 128), BF16), vm((16, CHUNK, 128), BF16),
+        dma((8,)), dma((4,)), dma((2, 12)), dma((2, 12)),
+        dma((8,)), dma((8,)), dma((16,)), dma((16,)), dma((8,)), dma((8,)),
+        dma((8,)), dma((8,)), dma((16,)), dma((16,)),
     ]
-    here = pl.BlockSpec(memory_space=pltpu.VMEM)
     there = pl.BlockSpec(memory_space=pl.ANY)
     params = dict(vmem_limit_bytes=60 * 1024 * 1024)
     if n_sx > 1:
@@ -582,7 +612,7 @@
         functools.partial(kernel, sizes, factor),
         out_shape=(jax.ShapeDtypeStruct(tile, BF16), jax.ShapeDtypeStruct(sums, F32)),
         in_specs=[there] * 6,
-        out_specs=(there, here),
+        out_specs=(there, there),
         scratch_shapes=scratch,
         compiler_params=pltpu.CompilerParams(**params),
         name="block",
@@ -603,9 +633,13 @@
             jax.ShapeDtypeStruct((1, CH), F32),
             jax.ShapeDtypeStruct((CH, CH), F32),
         ),
-        in_specs=[there, here],
-        out_specs=(there, here, here, here, here),
-        scratch_shapes=[vm(tile, BF16), dma((2, 4))],
+        in_specs=[there] * 2,
+        out_specs=(there,) * 5,
+        scratch_shapes=[
+            vm(tile, BF16), vm(sums.shape, F32), vm((27, CH), F32), vm((CH, CH), F32), vm((1, CH), F32),
+            vm((CH, CH), F32), dma((2, 8)),
+        ],
+        compiler_params=pltpu.CompilerParams(vmem_limit_bytes=60 * 1024 * 1024),
         name="deliver",
     )(ig, sums)
     return (ig.reshape(inputs.shape), kg.T, mig, bg.reshape(CH), mog)

time: 48 us -> 45.1 us (0.940)
  Pallas kernels: 47.1 us -> 44.3 us
    pallas_call x1, Pallas kernels: 43.2 us -> 41.7 us  [per_device(): pl.pallas_call(functools.partial(kernel, sizes, factor), out_shape=(jax.S...]
    pallas_call x1, Pallas kernels: 3.94 us -> 2.52 us  [per_device(): pl.pallas_call(deliver, out_shape=(jax.ShapeDtypeStruct(tile, BF16), jax....]
where the time goes in v3:
time: 45.1 us; the launch traced here: 44.9 us
  Pallas kernels  44.3 us (98%)
  between operations  0.64 us (1%)
    pallas_call x1, Pallas kernels, per_device(): pl.pallas_call(functools.partial(kernel, sizes, factor), out_shape=(jax.S...  41.7 us
    pallas_call x1, Pallas kernels, per_device(): pl.pallas_call(deliver, out_shape=(jax.ShapeDtypeStruct(tile, BF16), jax....  2.52 us

profile of v3, /device:TPU:1, one launch (start us, length us, event | category | flops | bytes accessed | tf_op | source)
XLA Modules:
  0.0 44.9 jit_solution(17076342164739137453)
XLA Ops:
  0.6 41.7 %block.1 = (bf16[192,2,16,128]{3,2,1,0:T(8,128)(2,1)}, f32[9,80,128]{2,1,0:T(8,128)}) custom-call(bf16[192,2,16,128]{3,2,1,0:T(8,128)(2,1)} %bitcast.7, bf16[192,2,16,128]{3,2,1,0:T(8,128)(2,1)} %bitcast.8, f32[27,192]{1,0:T(8,128)} %bitcast.9, f32[1,192]{1,0:T(1,128)} %bitcast.10, bf16[192,192]{1,0:T(8,128)(2,1)} %mi_hbm.1, bf16[192,192]{1,0:T(8,128)(2,1)} %mo_hbm.1), custom_call_target="tpu_custom_call" | custom-call | tf_op jit(solution)/shard_map/block/pallas_call | solution.py:611
  42.4 2.5 %deliver.1 = (bf16[192,2,16,128]{3,2,1,0:T(8,128)(2,1)}, f32[27,192]{1,0:T(8,128)}, f32[192,192]{1,0:T(8,128)}, f32[1,192]{1,0:T(1,128)}, f32[192,192]{1,0:T(8,128)}) custom-call(bf16[192,2,16,128]{3,2,1,0:T(8,128)(2,1)} %get-tuple-element.12.ig_in, f32[9,80,128]{2,1,0:T(8,128)} %get-tuple-element.13.sums_in), custom_call_target="tpu_custom_call" | custom-call | tf_op jit(solution)/shard_map/deliver/pallas_call | solution.py:627

commit v4 on v3

--- a/solution.py
+++ b/solution.py
@@ -46,11 +46,12 @@
 
 
 def rim_place(r, z):
-    if isinstance(r, int) and r == 0:
-        return 64 + 2 * z
-    if isinstance(r, int) and r == RR - 1:
-        return 68 + 2 * z
-    return 4 * (r - 1) + 2 * z
+    return 4 * r + 2 * z
+
+
+def swap_sides(packed):
+    even = iota(packed.shape, 1) % 2 == 0
+    return jnp.where(even, pltpu.roll(packed, 127, axis=1), pltpu.roll(packed, 1, axis=1))
 
 
 def pick_matrix():
@@ -86,12 +87,12 @@
     return (jnp.where(k == plus, 1.0, 0.0) - jnp.where(k == minus, 1.0, 0.0)).astype(BF16)
 
 
-def stencil_block(a0, am, ap, w, flip, rows, emit):
+def stencil_block(a0, am, ap, w, flip, rows, emit, first_row=0, last_row=RR - 1):
     k0 = [w[8 - t if flip else t, rows, :] for t in range(9)]
     kp = [w[18 + 8 - t if flip else 9 + t, rows, :] for t in range(9)]
     km = [w[9 + 8 - t if flip else 18 + t, rows, :] for t in range(9)]
     live = {}
-    for r in range(RR):
+    for r in range(first_row, last_row + 1):
         lower = [ref[r, 0, rows, :] for ref in (am, a0, ap)]
         upper = [ref[r, 1, rows, :] for ref in (am, a0, ap)]
         both = [u + v for u, v in zip(lower, upper)]
@@ -105,12 +106,32 @@
                 terms = (k0[t] * both[s], kp[t] * upper[s], km[t] * lower[s])
                 total = [b if a is None else a + b for a, b in zip(total, terms)]
             live[i] = total
-        if r >= 2:
-            shared, first, second = live.pop(r - 2)
-            emit(r - 2, shared + first, shared + second)
-
-
-def tap_sums_block(g0, a0, am, ap, rows):
+        for i in sorted(live):
+            if i + 2 == r or r == last_row:
+                shared, first, second = live.pop(i)
+                emit(i, shared + first, shared + second)
+
+
+def near_lanes(packed):
+    return {off: pltpu.roll(packed, (128 - off) % 128, axis=1) if off else packed for off in range(-2, 12, 2)}
+
+
+def tap_sums_block(g0, a0, am, ap, hx, gp, rows):
+    near = near_lanes(hx[rows, :])
+    grads = gp[rows, :]
+    lane = iota((BLK, NC), 1)
+    even = lane % 2 == 0
+    lower_grads = jnp.where(lane % 4 < 2, grads, 0.0)
+    upper_grads = grads - lower_grads
+    sums = [jnp.zeros((BLK, NC), F32)] * 27
+    for q in range(3):
+        up = lower_grads * near[4 * q + 2]
+        down = upper_grads * near[4 * q - 2]
+        for kind, value in ((0, grads * near[4 * q] + up + down), (1, up), (2, down)):
+            left = jnp.where(even, value, 0.0)
+            sums[9 * kind + 3 * q] = left
+            sums[9 * kind + 3 * q + 2] = value - left
+
     def step(r, sums):
         sums = list(sums)
         first = g0[r + 1, 0, rows, :]
@@ -126,7 +147,7 @@
                 sums[18 + t] = sums[18 + t] + second * lower
         return tuple(sums)
 
-    sums = lax.fori_loop(0, NR, step, tuple(jnp.zeros((BLK, NC), F32) for _ in range(27)), unroll=8)
+    sums = lax.fori_loop(0, NR, step, tuple(sums), unroll=8)
     middle = [sums[t] - sums[9 + t] - sums[18 + t] for t in range(9)]
     return list(sums[18:]) + middle + list(sums[9:18])
 
@@ -137,7 +158,7 @@
     ig_hbm, sums_hbm,
     xv, cv, ov, sums_ref, dk, bias, mi, mo,
     xb, hb, a0, am, ap, b0, bm, bp, cb, ag, hid, w, acc, mit, mot, turn, swap,
-    px, ph, prx, prh, edge, halo, moa, mia, tall, flat, gs, ar, br, fin, bs, pgs, ks, kr, kt, kg,
+    px, ph, prx, prh, edge, halo, hx, fx, gp, fw, moa, mia, tall, flat, gs, ar, br, fin, bs, pgs, ks, kr, kt, kg,
     load, save, hsend, hrecv, asend, arecv, bsend, brecv, csend, crecv, ksend, krecv, lsend, lrecv,
 ):
     n_sx, n_sy, n_sample = sizes
@@ -163,7 +184,7 @@
         for k, (src, dst) in enumerate(((mi_hbm, mi), (mo_hbm, mo), (dk_hbm, dk), (bias_hbm, bias), (cot_hbm, cv)))
     ]
     with jax.named_scope("start"):
-        for copy in loads[:7]:
+        for copy in loads[3:7] + loads[:3]:
             copy.start()
         if comm:
             barrier = pltpu.get_barrier_semaphore()
@@ -210,22 +231,32 @@
             ok = (sx + dx >= 0) & (sx + dx < n_sx) & (sy + dy >= 0) & (sy + dy < n_sy)
             return jnp.where(ok, recv[slot, block].astype(F32), 0.0)
 
-        row = iota((16, CH), 0)
-        left = row % 2 == 0
+        left = iota((16, CH), 0) % 2 == 0
         tall = [jnp.where(left, piece(0, k, 0, -1), piece(3, k, 0, 1)) for k in range(4)]
-        top = jnp.where(left, piece(1, 0, -1, -1), piece(4, 0, -1, 1))[8:16]
-        end = jnp.where(left, piece(2, 0, 1, -1), piece(5, 0, 1, 1))[0:8]
-        tall.append(pltpu.roll(jnp.where(row[0:8] >= 4, top, end), 4, axis=0))
-        tall.append(jnp.zeros((128 - 72, CH), F32))
+        tall.append(jnp.where(left, piece(2, 0, 1, -1), piece(5, 0, 1, 1)))
+        tall.append(jnp.zeros((32, CH), F32))
+        tall.append(jnp.where(left, piece(1, 0, -1, -1), piece(4, 0, -1, 1)))
         square = jnp.concatenate(tall, axis=0)
         square = jnp.concatenate([square, jnp.zeros((128, 64), F32)], axis=1)
-        return square.T[:CH].astype(BF16)
+        return pltpu.roll(square.T[:CH], 4, axis=1)
+
+    def edge_lanes():
+        square = jnp.concatenate([edge[...].reshape(64, CH), jnp.zeros((64, CH), F32)], axis=0)
+        square = jnp.concatenate([square, jnp.zeros((128, 64), F32)], axis=1)
+        return square.T[:CH]
+
+    def real_row(rows_ref, r):
+        ok = sx > 0 if r == 0 else sx < n_sx - 1
+        return jnp.where(ok, rows_ref[r].astype(F32), 0.0).astype(BF16)
+
+    def spread_plain(value, mid, back, ahead, r):
+        mid[r] = value.astype(F32)
+        both = dot(value.reshape(2 * CH, NC), turn[...])
+        back[r] = both[:, :NC].reshape(2, CH, NC)
+        ahead[r] = both[:, NC:].reshape(2, CH, NC)
 
     def spread(rows_ref, mid, back, ahead, r, z):
-        value = rows_ref[r, z]
-        if isinstance(r, int):
-            ok = sx > 0 if r == 0 else sx < n_sx - 1
-            value = jnp.where(ok, value.astype(F32), 0.0).astype(BF16)
+        value = real_row(rows_ref, r)[z] if isinstance(r, int) else rows_ref[r, z]
         mid[r, z] = value.astype(F32)
         lhs = jnp.concatenate([value, halo[...]], axis=1)
         rhs = jnp.concatenate([turn[...], rim_matrix(rim_place(r, z))], axis=0)
@@ -237,7 +268,7 @@
         if comm:
             for slot in range(6):
                 pack_copy(which, sent, recv, slot).wait_recv()
-            halo[...] = rim(recv)
+            halo[...] = rim(recv).astype(BF16)
         else:
             halo[...] = jnp.zeros_like(halo)
 
@@ -257,8 +288,37 @@
             for z in range(2):
                 spread(rows_ref, mid, back, ahead, r, z)
 
+    with jax.named_scope("constants"):
+        for k in range(3, 7):
+            loads[k].wait()
+        turn[...] = shift_matrix()
+        swap[...] = swap_matrix()
+        eye = one_hot(iota((CH, CH), 0) == iota((CH, CH), 1))
+        mit[...] = dot_nt(eye, mi[...]).astype(BF16)
+        mot[...] = dot_nt(eye, mo[...]).astype(BF16)
+
+    with jax.named_scope("weights"):
+        value = jnp.concatenate([dk[...], bias[...], jnp.zeros((100, CH), F32)], axis=0)
+        value = jnp.concatenate([value, jnp.zeros((128, 64), F32)], axis=1).T[:CH]
+        high = value.astype(BF16).astype(F32)
+        middle = (value - high).astype(BF16).astype(F32)
+        low = value - high - middle
+        tall[...] = (high + pltpu.roll(middle, 32, axis=1) + pltpu.roll(low, 64, axis=1)).astype(BF16)
+
+        @pl.loop(0, 14, unroll=7)
+        def _(d):
+            both = dot(tall[...], tap_matrix(d))
+            w[2 * d] = both[:, :128]
+            w[2 * d + 1] = both[:, 128:]
+
+        even = iota((CH, 128), 1) % 2 == 0
+        below = iota((CH, 128), 1) % 4 < 2
+        for q in range(3):
+            own, up, down = (jnp.where(even, w[9 * k + 3 * q], w[9 * k + 3 * q + 2]) for k in range(3))
+            fw[2 * q] = own
+            fw[2 * q + 1] = own + jnp.where(below, up, down)
+
     with jax.named_scope("rows of x"):
-        swap[...] = swap_matrix()
         for k in range(3):
             loads[k].wait()
 
@@ -286,31 +346,14 @@
         pack_edges(px)
         send_edges(0, px, prx)
 
-    with jax.named_scope("constants"):
-        for k in range(3, 7):
-            loads[k].wait()
-        turn[...] = shift_matrix()
-        eye = one_hot(iota((CH, CH), 0) == iota((CH, CH), 1))
-        mit[...] = dot_nt(eye, mi[...]).astype(BF16)
-        mot[...] = dot_nt(eye, mo[...]).astype(BF16)
-
-    with jax.named_scope("weights"):
-        value = jnp.concatenate([dk[...], bias[...], jnp.zeros((100, CH), F32)], axis=0)
-        value = jnp.concatenate([value, jnp.zeros((128, 64), F32)], axis=1).T[:CH]
-        high = value.astype(BF16).astype(F32)
-        middle = (value - high).astype(BF16).astype(F32)
-        low = value - high - middle
-        tall[...] = (high + pltpu.roll(middle, 32, axis=1) + pltpu.roll(low, 64, axis=1)).astype(BF16)
-
-        @pl.loop(0, 14, unroll=7)
-        def _(d):
-            both = dot(tall[...], tap_matrix(d))
-            w[2 * d] = both[:, :128]
-            w[2 * d + 1] = both[:, 128:]
+    with jax.named_scope("spread x"):
+        @pl.loop(1, NR + 1, unroll=8)
+        def _(r):
+            spread_plain(xb[r], a0, am, ap, r)
 
     loads[7].wait()
     with jax.named_scope("cotangent"):
-        @pl.loop(0, CH // WIDE, unroll=4)
+        @pl.loop(0, CH // WIDE, unroll=12)
         def _(b):
             part = cv[block_of(b, WIDE)]
             rhs = jnp.concatenate([part[:, z].reshape(WIDE * NR, NC) for z in range(2)], axis=1)
@@ -318,13 +361,6 @@
             for i in range(NR):
                 cb[i // 2, block_of(b, WIDE), 256 * (i % 2) : 256 * (i % 2) + 256] = both[WIDE * i : WIDE * (i + 1)]
 
-        @pl.loop(0, NR // 2, unroll=4)
-        def _(i):
-            ag[i] = dot(mot[...], cb[i])
-
-    with jax.named_scope("spread x"):
-        spread_all(0, xb, a0, am, ap, px, prx)
-
     with jax.named_scope("hidden"):
         @pl.loop(0, CH // BLK)
         def _(b):
@@ -335,21 +371,65 @@
                 hid[i // 2, rows, at : at + 128] = first
                 hid[i // 2, rows, at + 128 : at + 256] = second
 
-            stencil_block(a0, am, ap, w, False, rows, emit)
+            stencil_block(a0, am, ap, w, False, rows, emit, 1, NR)
+
+    with jax.named_scope("halo x"):
+        if comm:
+            for slot in range(6):
+                pack_copy(0, px, prx, slot).wait_recv()
+            hx[...] = rim(prx)
+            for k in range(3):
+                slab_copy(0, xb, 0, k).wait_recv()
+                slab_copy(0, xb, 1, k).wait_recv()
+        else:
+            hx[...] = jnp.zeros_like(hx)
+            xb[0] = jnp.zeros_like(xb[0])
+            xb[NR + 1] = jnp.zeros_like(xb[0])
+        for r in (0, NR + 1):
+            spread_plain(real_row(xb, r), a0, am, ap, r)
+
+        @pl.loop(0, CH // BLK, unroll=4)
+        def _(b):
+            rows = block_of(b, BLK)
+            for r, i, t0 in ((0, 0, 0), (NR + 1, NR - 1, 6)):
+                shared, first, second = 0.0, 0.0, 0.0
+                for s, ref in enumerate((am, a0, ap)):
+                    lower = ref[r, 0, rows, :]
+                    upper = ref[r, 1, rows, :]
+                    shared = shared + w[t0 + s, rows, :] * (lower + upper)
+                    first = first + w[9 + t0 + s, rows, :] * upper
+                    second = second + w[18 + t0 + s, rows, :] * lower
+                at = 256 * (i % 2)
+                hid[i // 2, rows, at : at + 128] += shared + first
+                hid[i // 2, rows, at + 128 : at + 256] += shared + second
+
+            below = iota((BLK, 128), 1) % 4 < 2
+            near = near_lanes(hx[rows, :])
+            total = 0.0
+            for q in range(3):
+                total = total + fw[2 * q, rows, :] * near[4 * q]
+                total = total + fw[2 * q + 1, rows, :] * jnp.where(below, near[4 * q + 2], near[4 * q - 2])
+            fx[rows, :] = swap_sides(total)
 
     with jax.named_scope("chain"):
         moa[...] = jnp.zeros_like(moa)
         mia[...] = jnp.zeros_like(mia)
 
-        @pl.loop(0, NR // 2, unroll=4)
+        @pl.loop(0, NR // 2, unroll=8)
         def _(i):
-            hidden = hid[i].astype(BF16)
+            column = iota((CH, NC), 1)
+            outer = (column == 0) | (column == NC - 1)
+            hidden = []
+            for k in range(4):
+                add = jnp.where(outer, pltpu.roll(fx[...], NC - 1 - 8 * i - 2 * k, axis=1), 0.0)
+                hidden.append((hid[i, :, NC * k : NC * (k + 1)] + add).astype(BF16))
+            hidden = jnp.concatenate(hidden, axis=1)
             shift = w[27]
             pre = dot(mi[...], hidden) + jnp.concatenate([shift] * 4, axis=1)
             cdf = 0.5 * (1.0 + lax.erf(pre * INV_SQRT2))
             dens = jnp.exp(-0.5 * pre * pre) * INV_SQRT2PI
             act = (pre * cdf).astype(BF16)
-            pg = (ag[i] * (cdf + pre * dens)).astype(BF16)
+            pg = (dot(mot[...], cb[i]) * (cdf + pre * dens)).astype(BF16)
             moa[...] += dot_nt(cb[i], act)
             mia[...] += dot_nt(pg, jnp.concatenate([hidden, jnp.ones((16, 4 * NC), BF16)], axis=0))
             pgs[i] = pg
@@ -428,7 +508,7 @@
                 scatter(d).start()
 
     with jax.named_scope("hidden grad"):
-        @pl.loop(0, NR // 2, unroll=4)
+        @pl.loop(0, NR // 2, unroll=8)
         def _(i):
             hg = dot(mit[...], pgs[i]).astype(BF16)
             for k in range(4):
@@ -449,15 +529,16 @@
         @pl.loop(start, stop)
         def _(b):
             rows = block_of(b, BLK)
-            for k, value in enumerate(tap_sums_block(b0, a0, am, ap, rows)):
+            for k, value in enumerate(tap_sums_block(b0, a0, am, ap, hx, gp, rows)):
                 acc[k, rows, :] = value
 
     with jax.named_scope("tap sums"):
-        tap_sums(0, 14)
+        gp[...] = swap_sides(edge_lanes())
+        tap_sums(0, 20)
     with jax.named_scope("sum sx"):
         sum_sx()
     with jax.named_scope("tap sums 2"):
-        tap_sums(14, 24)
+        tap_sums(20, 24)
         acc[27] = jnp.where(iota((CH, NC), 1) == 0, mia[:, 192:193], 0.0)
 
         for k in range(28):
@@ -477,8 +558,8 @@
     with jax.named_scope("spread grad"):
         spread_all(1, hb, b0, bm, bp, ph, prh)
 
-    def input_grad(part):
-        @pl.loop(8 * part, 8 * part + 8)
+    def input_grad(start, stop):
+        @pl.loop(2 * start, 2 * stop)
         def _(b):
             rows = block_of(b, BLK)
 
@@ -489,7 +570,7 @@
 
             stencil_block(b0, bm, bp, w, True, rows, emit)
 
-        @pl.loop(4 * part, 4 * part + 4, unroll=4)
+        @pl.loop(start, stop, unroll=stop - start)
         def _(b):
             rows = block_of(b, WIDE)
             rhs = [ag[i // 2, rows, 256 * (i % 2) : 256 * (i % 2) + 256].astype(BF16) for i in range(NR)]
@@ -503,16 +584,19 @@
         return pltpu.make_async_copy(ov.at[at], ig_hbm.at[at], save.at[part])
 
     with jax.named_scope("grad 1"):
-        input_grad(0)
-    save_part(0).start()
+        input_grad(0, 3)
     with jax.named_scope("sum rest"):
         sum_taps()
+    with jax.named_scope("grad 2"):
+        input_grad(3, 5)
+    with jax.named_scope("sum rest 2"):
         sum_group()
-    with jax.named_scope("grad 2"):
-        input_grad(1)
+    with jax.named_scope("grad 3"):
+        input_grad(5, 8)
+    save_part(0).start()
     save_part(1).start()
-    with jax.named_scope("grad 3"):
-        input_grad(2)
+    with jax.named_scope("grad 4"):
+        input_grad(8, 12)
     save_part(2).start()
 
     with jax.named_scope("finish"):
@@ -596,6 +680,7 @@
         vm((CH, CH), BF16), vm((CH, CH), BF16), vm((NC, 2 * NC), BF16), vm((256, 256), BF16),
         vm((4, 16, CH), BF16), vm((4, 16, CH), BF16), vm((6, 4, 16, CH), BF16), vm((6, 4, 16, CH), BF16),
         vm((NR // 2, 8, CH), F32), vm((CH, 128), BF16),
+        vm((CH, 128), F32), vm((CH, 128), F32), vm((CH, 128), F32), vm((6, CH, 128), F32),
         vm((CH, CH), F32), vm((CH, CH + 16), F32), vm((CH, 128), BF16), vm((28, 8, CH), F32),
         vm((PARTS, PIECE, 128), BF16), vm((PARTS, PIECE, 128), BF16), vm((16, PIECE, 128), BF16),
         vm((PARTS, PIECE, 128), BF16), vm((PIECE, 128), BF16), vm(pairs, BF16),

time: 45.1 us -> 43.4 us (0.962)
  Pallas kernels: 44.3 us -> 42.6 us
    pallas_call x1, Pallas kernels: 41.7 us -> 40.1 us  [per_device(): pl.pallas_call(functools.partial(kernel, sizes, factor), out_shape=(jax.S...]
where the time goes in v4:
time: 43.4 us; the launch traced here: 43.3 us
  Pallas kernels  42.6 us (98%)
  between operations  0.64 us (1%)
    pallas_call x1, Pallas kernels, per_device(): pl.pallas_call(functools.partial(kernel, sizes, factor), out_shape=(jax.S...  40.1 us
    pallas_call x1, Pallas kernels, per_device(): pl.pallas_call(deliver, out_shape=(jax.ShapeDtypeStruct(tile, BF16), jax....  2.52 us

profile of v4, /device:TPU:1, one launch (start us, length us, event | category | flops | bytes accessed | tf_op | source)
XLA Modules:
  0.0 43.3 jit_solution(13942694803928430013)
XLA Ops:
  0.6 40.1 %block.1 = (bf16[192,2,16,128]{3,2,1,0:T(8,128)(2,1)}, f32[9,80,128]{2,1,0:T(8,128)}) custom-call(bf16[192,2,16,128]{3,2,1,0:T(8,128)(2,1)} %bitcast.7, bf16[192,2,16,128]{3,2,1,0:T(8,128)(2,1)} %bitcast.8, f32[27,192]{1,0:T(8,128)} %bitcast.9, f32[1,192]{1,0:T(1,128)} %bitcast.10, bf16[192,192]{1,0:T(8,128)(2,1)} %mi_hbm.1, bf16[192,192]{1,0:T(8,128)(2,1)} %mo_hbm.1), custom_call_target="tpu_custom_call" | custom-call | tf_op jit(solution)/shard_map/block/pallas_call | solution.py:696
  40.8 2.5 %deliver.1 = (bf16[192,2,16,128]{3,2,1,0:T(8,128)(2,1)}, f32[27,192]{1,0:T(8,128)}, f32[192,192]{1,0:T(8,128)}, f32[1,192]{1,0:T(1,128)}, f32[192,192]{1,0:T(8,128)}) custom-call(bf16[192,2,16,128]{3,2,1,0:T(8,128)(2,1)} %get-tuple-element.12.ig_in, f32[9,80,128]{2,1,0:T(8,128)} %get-tuple-element.13.sums_in), custom_call_target="tpu_custom_call" | custom-call | tf_op jit(solution)/shard_map/deliver/pallas_call | solution.py:712

commit v5 on v4

--- a/solution.py
+++ b/solution.py
@@ -153,12 +153,12 @@
 
 
 def kernel(
-    sizes, factor,
+    sizes,
     x_hbm, cot_hbm, dk_hbm, bias_hbm, mi_hbm, mo_hbm,
-    ig_hbm, sums_hbm,
-    xv, cv, ov, sums_ref, dk, bias, mi, mo,
+    ig_hbm, fin, kg,
+    xv, cv, ov, dk, bias, mi, mo,
     xb, hb, a0, am, ap, b0, bm, bp, cb, ag, hid, w, acc, mit, mot, turn, swap,
-    px, ph, prx, prh, edge, halo, hx, fx, gp, fw, moa, mia, tall, flat, gs, ar, br, fin, bs, pgs, ks, kr, kt, kg,
+    px, ph, prx, prh, edge, halo, hx, fx, gp, fw, moa, mia, tall, flat, gs, ar, br, fo, bs, pgs, ks, kr, kt,
     load, save, hsend, hrecv, asend, arecv, bsend, brecv, csend, crecv, ksend, krecv, lsend, lrecv,
 ):
     n_sx, n_sy, n_sample = sizes
@@ -388,7 +388,7 @@
         for r in (0, NR + 1):
             spread_plain(real_row(xb, r), a0, am, ap, r)
 
-        @pl.loop(0, CH // BLK, unroll=4)
+        @pl.loop(0, CH // BLK, unroll=8)
         def _(b):
             rows = block_of(b, BLK)
             for r, i, t0 in ((0, 0, 0), (NR + 1, NR - 1, 6)):
@@ -450,7 +450,7 @@
         return over_sx(gs.at[lax.rem(sx + d, n_sx)], ar, asend, arecv, d)
 
     def publish(d):
-        return over_sx(fin.at[sx], fin, csend, crecv, d)
+        return over_sx(fo, fin, csend, crecv, d)
 
     def arrived(ref, sem, slot):
         pltpu.make_async_remote_copy(
@@ -471,6 +471,12 @@
         for k in range(1, count):
             total = total + ref[k].astype(F32)
         return total
+
+    def own_mixes():
+        return pltpu.make_async_copy(fo, fin.at[sx], save.at[3])
+
+    def own_taps():
+        return pltpu.make_async_copy(kt, kg.at[me], save.at[4])
 
     def sum_sx():
         if comm:
@@ -484,9 +490,10 @@
     def sum_group():
         if comm:
             arrived_group(br, brecv)
-            fin[sx] = added(br, n_group).astype(BF16)
+            fo[...] = added(br, n_group).astype(BF16)
             for d in range(1, n_sx):
                 publish(d).start()
+            own_mixes().start()
 
     def sum_taps():
         if comm:
@@ -495,7 +502,7 @@
             kt[...] = added(kr, n_sx).astype(BF16)
             for d in range(1, n_group):
                 over_group(kt, kg, lsend, lrecv, d).start()
-            kg[me] = kt[...]
+            own_taps().start()
 
     with jax.named_scope("scatter mixes"):
         for k in range(PARTS):
@@ -534,11 +541,11 @@
 
     with jax.named_scope("tap sums"):
         gp[...] = swap_sides(edge_lanes())
-        tap_sums(0, 20)
+        tap_sums(0, 16)
     with jax.named_scope("sum sx"):
         sum_sx()
     with jax.named_scope("tap sums 2"):
-        tap_sums(20, 24)
+        tap_sums(16, 24)
         acc[27] = jnp.where(iota((CH, NC), 1) == 0, mia[:, 192:193], 0.0)
 
         for k in range(28):
@@ -616,40 +623,41 @@
                 over_group(kt, kg, lsend, lrecv, d).wait_send()
             arrived_sx(fin, crecv)
             arrived_group(kg, lrecv)
-            sums_ref[PARTS, 0:CHUNK] = added(kg, n_group) * factor
-        else:
-            fin[...] = gs[...]
-            sums_ref[PARTS, 0:CHUNK] = ks[...].astype(F32) * factor
-        sums_ref[PARTS, CHUNK:PIECE] = jnp.zeros((PIECE - CHUNK, 128), F32)
-        sums_ref[0:PARTS] = fin[...].astype(F32) * factor
-        last = pltpu.make_async_copy(sums_ref, sums_hbm, save.at[3])
-        last.start()
+            own_mixes().wait()
+            own_taps().wait()
         for part in range(3):
             save_part(part).wait()
-        last.wait()
-
-
-def deliver(ig_in, sums_in, ig_out, kg_out, mig_out, bg_out, mog_out, held, sums, kg, mig, bg, mog, sems):
+
+
+def deliver(factor, n_group, ig_in, fin_in, kg_in, ig_out, kg_out, mig_out, bg_out, mog_out, held, fin, taps, kg, mig, bg, mog, sems):
     parts = CH // 4
     at = [pl.ds(parts * k, parts) for k in range(4)]
     inward = [pltpu.make_async_copy(ig_in.at[at[k]], held.at[at[k]], sems.at[0, k]) for k in range(4)]
     outward = [pltpu.make_async_copy(held.at[at[k]], ig_out.at[at[k]], sems.at[1, k]) for k in range(4)]
-    first = pltpu.make_async_copy(sums_in, sums, sems.at[0, 4])
+    first = pltpu.make_async_copy(fin_in, fin, sems.at[0, 4])
+    second = pltpu.make_async_copy(kg_in, taps, sems.at[0, 5])
     first.start()
+    second.start()
     for copy in inward:
         copy.start()
     first.wait()
     for k in range(PARTS):
         rows = pl.ds(24 * k, 24)
-        mog[rows, 0:128] = sums[k, 0:24]
-        mog[rows, 128:192] = sums[k, 24:48, 0:64]
-        mig[rows, 0:64] = sums[k, 24:48, 64:128]
-        mig[rows, 64:192] = sums[k, 48:72]
-    kg[:, 0:128] = sums[PARTS, 0:27]
-    kg[0:16, 128:192] = sums[PARTS, 32:48, 0:64]
-    kg[16:27, 128:192] = sums[PARTS, 32:43, 64:128]
-    bg[:, 0:128] = sums[PARTS, 27:28]
-    bg[:, 128:192] = sums[PARTS, 43:44, 64:128]
+        value = fin[k].astype(F32) * factor
+        mog[rows, 0:128] = value[0:24]
+        mog[rows, 128:192] = value[24:48, 0:64]
+        mig[rows, 0:64] = value[24:48, 64:128]
+        mig[rows, 64:192] = value[48:72]
+    second.wait()
+    value = taps[0].astype(F32)
+    for g in range(1, n_group):
+        value = value + taps[g].astype(F32)
+    value = value * factor
+    kg[:, 0:128] = value[0:27]
+    kg[0:16, 128:192] = value[32:48, 0:64]
+    kg[16:27, 128:192] = value[32:43, 64:128]
+    bg[:, 0:128] = value[27:28]
+    bg[:, 128:192] = value[43:44, 64:128]
     pairs = ((kg, kg_out), (mig, mig_out), (bg, bg_out), (mog, mog_out))
     small = [pltpu.make_async_copy(src, dst, sems.at[1, 4 + k]) for k, (src, dst) in enumerate(pairs)]
     for copy in small:
@@ -668,9 +676,10 @@
     pairs = (NR // 2, CH, 4 * NC)
     dma = pltpu.SemaphoreType.DMA
     n_sx, n_sy, n_sample = sizes
-    sums = (PARTS + 1, PIECE, 128)
+    mixes = (PARTS, PIECE, 128)
+    taps = (16, CHUNK, 128)
     scratch = [
-        vm(tile, BF16), vm(tile, BF16), vm(tile, BF16), vm(sums, F32),
+        vm(tile, BF16), vm(tile, BF16), vm(tile, BF16),
         vm((27, CH), F32), vm((1, CH), F32), vm((CH, CH), BF16), vm((CH, CH), BF16),
         vm(field, BF16), vm(field, BF16),
         vm(field, F32), vm(field, F32), vm(field, F32),
@@ -683,9 +692,9 @@
         vm((CH, 128), F32), vm((CH, 128), F32), vm((CH, 128), F32), vm((6, CH, 128), F32),
         vm((CH, CH), F32), vm((CH, CH + 16), F32), vm((CH, 128), BF16), vm((28, 8, CH), F32),
         vm((PARTS, PIECE, 128), BF16), vm((PARTS, PIECE, 128), BF16), vm((16, PIECE, 128), BF16),
-        vm((PARTS, PIECE, 128), BF16), vm((PIECE, 128), BF16), vm(pairs, BF16),
-        vm((CHUNK, 128), BF16), vm((8, CHUNK, 128), BF16), vm((CHUNK, 128), BF16), vm((16, CHUNK, 128), BF16),
-        dma((8,)), dma((4,)), dma((2, 12)), dma((2, 12)),
+        vm((PIECE, 128), BF16), vm((PIECE, 128), BF16), vm(pairs, BF16),
+        vm((CHUNK, 128), BF16), vm((8, CHUNK, 128), BF16), vm((CHUNK, 128), BF16),
+        dma((8,)), dma((5,)), dma((2, 12)), dma((2, 12)),
         dma((8,)), dma((8,)), dma((16,)), dma((16,)), dma((8,)), dma((8,)),
         dma((8,)), dma((8,)), dma((16,)), dma((16,)),
     ]
@@ -693,11 +702,11 @@
     params = dict(vmem_limit_bytes=60 * 1024 * 1024)
     if n_sx > 1:
         params.update(collective_id=0, has_side_effects=True)
-    ig, sums = pl.pallas_call(
-        functools.partial(kernel, sizes, factor),
-        out_shape=(jax.ShapeDtypeStruct(tile, BF16), jax.ShapeDtypeStruct(sums, F32)),
+    ig, fin, kg = pl.pallas_call(
+        functools.partial(kernel, sizes),
+        out_shape=tuple(jax.ShapeDtypeStruct(shape, BF16) for shape in (tile, mixes, taps)),
         in_specs=[there] * 6,
-        out_specs=(there, there),
+        out_specs=(there,) * 3,
         scratch_shapes=scratch,
         compiler_params=pltpu.CompilerParams(**params),
         name="block",
@@ -710,7 +719,7 @@
         mix_out,
     )
     ig, kg, mig, bg, mog = pl.pallas_call(
-        deliver,
+        functools.partial(deliver, factor, n_sy * n_sample),
         out_shape=(
             jax.ShapeDtypeStruct(tile, BF16),
             jax.ShapeDtypeStruct((27, CH), F32),
@@ -718,15 +727,15 @@
             jax.ShapeDtypeStruct((1, CH), F32),
             jax.ShapeDtypeStruct((CH, CH), F32),
         ),
-        in_specs=[there] * 2,
+        in_specs=[there] * 3,
         out_specs=(there,) * 5,
         scratch_shapes=[
-            vm(tile, BF16), vm(sums.shape, F32), vm((27, CH), F32), vm((CH, CH), F32), vm((1, CH), F32),
+            vm(tile, BF16), vm(mixes, BF16), vm(taps, BF16), vm((27, CH), F32), vm((CH, CH), F32), vm((1, CH), F32),
             vm((CH, CH), F32), dma((2, 8)),
         ],
         compiler_params=pltpu.CompilerParams(vmem_limit_bytes=60 * 1024 * 1024),
         name="deliver",
-    )(ig, sums)
+    )(ig, fin, kg)
     return (ig.reshape(inputs.shape), kg.T, mig, bg.reshape(CH), mog)
 
 

time: 43.4 us -> 42.4 us (0.977)
  Pallas kernels: 42.6 us -> 41.6 us
    pallas_call x2, Pallas kernels: 42.6 us -> 41.6 us  [the longest x1 39 us: per_device(): pl.pallas_call(functools.partial(kernel, sizes), out_shape=tuple((jax.Sha...]
where the time goes in v5:
time: 42.4 us; the launch traced here: 42.2 us
  Pallas kernels  41.6 us (98%)
  between operations  0.64 us (2%)
    pallas_call x1, Pallas kernels, per_device(): pl.pallas_call(functools.partial(kernel, sizes), out_shape=tuple((jax.Sha...  39 us
    pallas_call x1, Pallas kernels, per_device(): pl.pallas_call(functools.partial(deliver, factor, n_sy * n_sample), out_s...  2.55 us

profile of v5, /device:TPU:1, one launch (start us, length us, event | category | flops | bytes accessed | tf_op | source)
XLA Modules:
  0.0 42.2 jit_solution(6692097764746661279)
XLA Ops:
  0.6 39.0 %block.1 = (bf16[192,2,16,128]{3,2,1,0:T(8,128)(2,1)}, bf16[8,80,128]{2,1,0:T(8,128)(2,1)}, bf16[16,48,128]{2,1,0:T(8,128)(2,1)}) custom-call(bf16[192,2,16,128]{3,2,1,0:T(8,128)(2,1)} %bitcast.7, bf16[192,2,16,128]{3,2,1,0:T(8,128)(2,1)} %bitcast.8, f32[27,192]{1,0:T(8,128)} %bitcast.9, f32[1,192]{1,0:T(1,128)} %bitcast.10, bf16[192,192]{1,0:T(8,128)(2,1)} %mi_hbm.1, ...), custom_call_target="tpu_custom_call" | custom-call | tf_op jit(solution)/shard_map/block/pallas_call | solution.py:705
  39.7 2.6 %deliver.1 = (bf16[192,2,16,128]{3,2,1,0:T(8,128)(2,1)}, f32[27,192]{1,0:T(8,128)}, f32[192,192]{1,0:T(8,128)}, f32[1,192]{1,0:T(1,128)}, f32[192,192]{1,0:T(8,128)}) custom-call(bf16[192,2,16,128]{3,2,1,0:T(8,128)(2,1)} %get-tuple-element.13.ig_in, bf16[8,80,128]{2,1,0:T(8,128)(2,1)} %get-tuple-element.14.fin_in, bf16[16,48,128]{2,1,0:T(8,128)(2,1)} %get-tuple-element.15.kg_in), custom_call_target="tpu_custom_call" | custom-call | tf_op jit(solution)/shard_map/deliver/pallas_call | solution.py:721

commit v6 on v5

--- a/solution.py
+++ b/solution.py
@@ -362,7 +362,7 @@
                 cb[i // 2, block_of(b, WIDE), 256 * (i % 2) : 256 * (i % 2) + 256] = both[WIDE * i : WIDE * (i + 1)]
 
     with jax.named_scope("hidden"):
-        @pl.loop(0, CH // BLK)
+        @pl.loop(0, CH // BLK, unroll=2)
         def _(b):
             rows = block_of(b, BLK)
 
@@ -533,7 +533,7 @@
         send_edges(1, ph, prh)
 
     def tap_sums(start, stop):
-        @pl.loop(start, stop)
+        @pl.loop(start, stop, unroll=2)
         def _(b):
             rows = block_of(b, BLK)
             for k, value in enumerate(tap_sums_block(b0, a0, am, ap, hx, gp, rows)):

time: 42.4 us -> 42.1 us (level)
  no operation moved by 1% of the time
where the time goes in v6:
time: 42.1 us; the launch traced here: 41.9 us
  Pallas kernels  41.3 us (98%)
  between operations  0.64 us (2%)
    pallas_call x1, Pallas kernels, per_device(): pl.pallas_call(functools.partial(kernel, sizes), out_shape=tuple((jax.Sha...  38.7 us
    pallas_call x1, Pallas kernels, per_device(): pl.pallas_call(functools.partial(deliver, factor, n_sy * n_sample), out_s...  2.55 us

profile of v6, /device:TPU:1, one launch (start us, length us, event | category | flops | bytes accessed | tf_op | source)
XLA Modules:
  0.0 41.9 jit_solution(10589385902075737922)
XLA Ops:
  0.6 38.7 %block.1 = (bf16[192,2,16,128]{3,2,1,0:T(8,128)(2,1)}, bf16[8,80,128]{2,1,0:T(8,128)(2,1)}, bf16[16,48,128]{2,1,0:T(8,128)(2,1)}) custom-call(bf16[192,2,16,128]{3,2,1,0:T(8,128)(2,1)} %bitcast.7, bf16[192,2,16,128]{3,2,1,0:T(8,128)(2,1)} %bitcast.8, f32[27,192]{1,0:T(8,128)} %bitcast.9, f32[1,192]{1,0:T(1,128)} %bitcast.10, bf16[192,192]{1,0:T(8,128)(2,1)} %mi_hbm.1, ...), custom_call_target="tpu_custom_call" | custom-call | tf_op jit(solution)/shard_map/block/pallas_call | solution.py:705
  39.4 2.6 %deliver.1 = (bf16[192,2,16,128]{3,2,1,0:T(8,128)(2,1)}, f32[27,192]{1,0:T(8,128)}, f32[192,192]{1,0:T(8,128)}, f32[1,192]{1,0:T(1,128)}, f32[192,192]{1,0:T(8,128)}) custom-call(bf16[192,2,16,128]{3,2,1,0:T(8,128)(2,1)} %get-tuple-element.13.ig_in, bf16[8,80,128]{2,1,0:T(8,128)(2,1)} %get-tuple-element.14.fin_in, bf16[16,48,128]{2,1,0:T(8,128)(2,1)} %get-tuple-element.15.kg_in), custom_call_target="tpu_custom_call" | custom-call | tf_op jit(solution)/shard_map/deliver/pallas_call | solution.py:721
